TPU v7x, 32 devices: a whole 2x2x4 slice. The times are simulated.
32 devices in a mesh: groups: 2 (over y), tile: 4 (over z), chan: 2 (over x), sub: 2 (over core).
Axes of the slice: x: 2, y: 2, z: 4, core: 2. Of those that a mesh axis runs over, the one named last changes fastest.
Arguments:
- cycle_maps: bfloat16 [8, 3, 65536], P(('groups', 'chan', 'sub'), None, 'tile'), parts along dimension 0, may hold values from -6 to 6
- send_pick: int32 [98304], P('tile'), may hold values from 0 to 16384, as said below
- recv_pick: int32 [65536], P('tile'), may hold values from 0 to 24575, as said below
- neighbour: int32 [4, 4], replicated, may hold values from -1 to 3, as said below
- facing: int32 [4, 4], replicated, may hold values from 0 to 3, as said below
- conv_first: bfloat16 [9, 64, 3], replicated, may hold values from -1.25 to 1.25
- conv_second: bfloat16 [9, 64, 64], replicated, may hold values from -0.25 to 0.25
- cotangent: bfloat16 [8, 64, 65536], P(('groups', 'chan', 'sub'), None, 'tile'), parts along dimension 0, may hold values from -6 to 6
Outputs:
- output_maps: bfloat16 [8, 64, 65536], P(('groups', 'chan', 'sub'), None, 'tile'), parts along dimension 0
- grad_hidden: bfloat16 [8, 64, 65536], P(('groups', 'chan', 'sub'), None, 'tile'), parts along dimension 0
- grad_first: float32 [18, 64, 3], P('groups'), parts along dimension 0
- grad_second: float32 [18, 64, 64], P('groups'), parts along dimension 0
There are 2 independent parts, one for each index of `groups`. A program takes and returns all parts, laid end to end along the dimension named above; an argument that names none is the same for every part. Nothing has to cross between parts.
Inputs may be any that keep to these rules, and one draw needn't show every extreme that they name: `send_pick`: entry ((i * 4) + d) * 6144 + s names the cycle pixel (0 to 16383, local to owner i) that owner i puts into slot s of its block for tile d, or 16384 for an empty slot; the used slots of each block are 0 to n - 1 with n at most 6144, and some block is full. Every cycle pixel is named exactly once. `recv_pick`: entry d * 16384 + q is i * 6144 + s: pixel q of tile d is carried in slot s of owner i's block for tile d, a used slot. With send_pick it maps cycle pixels one to one onto tile pixels; each tile receives from every owner. `neighbour`: the tiles form a band four tiles tall, closed east to west; each tile is turned by a multiple of a right angle. Row t lists the tile across sides north, east, south, west of tile t in its own orientation, -1 beyond the band's rim. Adjacency is mutual: if side k of t touches side j of p, side j of p touches side k of t. A tile meets one tile on at most 2 sides, and some tile on exactly that many. `facing`: the side of the neighbouring tile that touches side k of tile t; 0 where there is no neighbour.
All inputs are finite; a program needn't handle non-finite values.
Results may differ from a plain program's by a relative error of at most 0.005.
Values may be sent and summed in bfloat16 or wider, within the bound.
A program may use at most 192 MiB of HBM per device.

v0:
```python
import math

import jax
import jax.numpy as jnp
from jax import lax
from jax.sharding import PartitionSpec as P

SIDE = 128
CH = 64


def border(field):
    return jnp.stack([field[:, :, 0, :], field[:, :, :, -1], field[:, :, -1, :], field[:, :, :, 0]])


def frame_rim(frame):
    return jnp.stack(
        [frame[:, :, 0, 1:-1], frame[:, :, 1:-1, -1], frame[:, :, -1, 1:-1], frame[:, :, 1:-1, 0]]
    )


def outgoing(strips):
    return jnp.stack([strips[0], strips[1], strips[2][..., ::-1], strips[3][..., ::-1]])


def orient(strips):
    return jnp.stack([strips[0][..., ::-1], strips[1][..., ::-1], strips[2], strips[3]])


def with_rims(field, incoming):
    padded = jnp.pad(field, ((0, 0), (0, 0), (1, 1), (1, 1)))
    padded = padded.at[:, :, 0, 1:-1].set(incoming[0])
    padded = padded.at[:, :, 1:-1, -1].set(incoming[1])
    padded = padded.at[:, :, -1, 1:-1].set(incoming[2])
    padded = padded.at[:, :, 1:-1, 0].set(incoming[3])
    return padded


def add_rims(interior, incoming):
    interior = interior.at[:, :, 0, :].add(incoming[0])
    interior = interior.at[:, :, :, -1].add(incoming[1])
    interior = interior.at[:, :, -1, :].add(incoming[2])
    interior = interior.at[:, :, :, 0].add(incoming[3])
    return interior


def windows(padded, width, anchor):
    stacked = []
    for position in range(9):
        row_shift, col_shift = divmod(position, 3)
        row_start = (
            anchor + (2 - 2 * anchor) * row_shift // 2 if anchor == 0 else anchor - row_shift
        )
        col_start = (
            anchor + (2 - 2 * anchor) * col_shift // 2 if anchor == 0 else anchor - col_shift
        )
        stacked.append(padded[:, :, row_start : row_start + width, col_start : col_start + width])
    return jnp.stack(stacked, axis=1)


def weight_terms(columns, grad_out):
    return jnp.einsum("boij,bpcij->poc", grad_out, columns, preferred_element_type=jnp.float32)


def spread(grad_out, weights):
    wide = jnp.pad(grad_out, ((0, 0), (0, 0), (2, 2), (2, 2)))
    return jnp.einsum(
        "poc,bpoij->bcij", weights, windows(wide, SIDE + 2, 2), preferred_element_type=jnp.float32
    )


def pick_gathered(gathered, pick_table):
    return jnp.einsum(
        "kq,qbcs->kbcs", pick_table, gathered, preferred_element_type=jnp.float32
    ).astype(gathered.dtype)


def body(cycle_maps, send_pick, recv_pick, neighbour, facing, conv_first, conv_second, cotangent):
    map_count, input_count, pixel_count = cycle_maps.shape
    tile_count = lax.axis_size("tile")
    block_slots = send_pick.shape[0] // tile_count
    my_index = lax.axis_index("tile")
    devices = jnp.arange(tile_count, dtype=jnp.int32)
    sides = jnp.arange(4, dtype=jnp.int32)
    mine = (devices == my_index)[:, None]
    my_nbr = jnp.sum(jnp.where(mine, neighbour, 0), axis=0)
    my_face = jnp.sum(jnp.where(mine, facing, 0), axis=0)
    partner = my_nbr[:, None] == devices[None, :]
    facing_hot = my_face[:, None] == sides[None, :]
    pick_table = (
        (partner[:, :, None] & facing_hot[:, None, :])
        .reshape(4, 4 * tile_count)
        .astype(jnp.bfloat16)
    )
    extended = jnp.concatenate(
        [cycle_maps, jnp.zeros((map_count, input_count, 1), cycle_maps.dtype)], axis=2
    )
    blocks_out = jnp.take(extended, send_pick, axis=2).reshape(
        map_count, input_count, tile_count, block_slots
    )
    arrived = lax.all_to_all(blocks_out, "tile", split_axis=2, concat_axis=2, tiled=True)
    tiles = jnp.take(
        arrived.reshape(map_count, input_count, tile_count * block_slots), recv_pick, axis=2
    )
    tiles = tiles.reshape(map_count, input_count, SIDE, SIDE)
    incoming = pick_gathered(
        lax.all_gather(outgoing(border(tiles)), "tile", axis=0, tiled=True), pick_table
    )
    padded_in = with_rims(tiles, orient(incoming))
    input_columns = windows(padded_in, SIDE, 0)
    pre = jnp.einsum(
        "poc,bpcij->boij", conv_first, input_columns, preferred_element_type=jnp.float32
    )
    hidden = jax.nn.silu(pre).astype(jnp.bfloat16)
    incoming = pick_gathered(
        lax.all_gather(outgoing(border(hidden)), "tile", axis=0, tiled=True), pick_table
    )
    padded_hidden = with_rims(hidden, orient(incoming))
    hidden_columns = windows(padded_hidden, SIDE, 0)
    output_maps = jnp.einsum(
        "poc,bpcij->boij", conv_second, hidden_columns, preferred_element_type=jnp.float32
    ).astype(jnp.bfloat16)
    count = map_count * lax.axis_size("chan") * lax.axis_size("sub") * tile_count * SIDE * SIDE
    scale = 1.0 / math.sqrt(count)
    grad_out = cotangent.reshape(map_count, CH, SIDE, SIDE)
    second_term = weight_terms(hidden_columns, grad_out) * scale
    grad_frame = spread(grad_out, conv_second)
    rim_strips = outgoing(frame_rim(grad_frame)).astype(jnp.bfloat16)
    incoming = pick_gathered(lax.all_gather(rim_strips, "tile", axis=0, tiled=True), pick_table)
    hidden_grad = add_rims(grad_frame[:, :, 1:-1, 1:-1], orient(incoming).astype(jnp.float32))
    sigma = jax.nn.sigmoid(pre)
    pre_grad = (hidden_grad * sigma * (1.0 + pre * (1.0 - sigma))).astype(jnp.bfloat16)
    first_term = weight_terms(input_columns, pre_grad) * scale
    grad_first, grad_second = lax.psum((first_term, second_term), ("tile", "chan", "sub"))
    output_flat = output_maps.reshape(map_count, CH, pixel_count)
    grad_flat = hidden_grad.astype(jnp.bfloat16).reshape(map_count, CH, pixel_count)
    return (output_flat, grad_flat, grad_first, grad_second)


def solution(mesh):
    in_specs = (
        P(("groups", "chan", "sub"), None, "tile"),
        P("tile"),
        P("tile"),
        P(),
        P(),
        P(),
        P(),
        P(("groups", "chan", "sub"), None, "tile"),
    )
    out_specs = (
        P(("groups", "chan", "sub"), None, "tile"),
        P(("groups", "chan", "sub"), None, "tile"),
        P("groups", None, None),
        P("groups", None, None),
    )
    return jax.shard_map(body, mesh=mesh, in_specs=in_specs, out_specs=out_specs, check_vma=False)
```

profile of v0, /device:TPU:0, one launch (start us, length us, event | category | flops | bytes accessed | tf_op | source)
XLA Modules:
  0.0 563.1 jit_solution(10738026590723426309)
XLA Ops:
  9.1 4.1 copy.631
  13.1 5.4 pad_bitcast_fusion
  18.5 85.2 %gather_fusion = bf16[24576,3]{1,0:T(8,128)(2,1)} fusion(bf16[3,16385]{0,1:T(8,128)(2,1)} %pad_bitcast_fusion, s32[24576]{0:T(1024)S(1)} %fusion.91), kind=kCustom, calls=%fused_computation | custom fusion | bytes 393216 | tf_op jit(solution)/shard_map/jit(_take)/gather | solution.py:98
  103.7 5.3 copy.632
  110.0 6.3 %all-to-all-start = ((bf16[1,3,4,6144]{3,1,0,2:T(4,128)(2,1)}), bf16[1,3,4,6144]{3,1,0,2:T(4,128)(2,1)S(1)}, u32[]{:S(2)}, u32[]{:S(2)}) async-start(bf16[1,3,4,6144]{3,1,0,2:T(4,128)(2,1)} %broadcast_select_fusion), calls=%async_computation | async-start | bytes 393216 | tf_op jit(solution)/shard_map/all_to_all | solution.py:101
  119.8 3.7 fusion.9
  123.5 3.6 fusion.11
  129.9 3.6 fusion.15
  133.5 3.6 fusion.17
  137.1 2.8 fusion.19
  139.9 3.6 fusion.21
  143.4 3.6 fusion.23
  147.0 19.4 %fusion = f32[130,130,64,1]{1,2,3,0:T(8,128)} fusion(bf16[1,9,64,130,130]{4,2,1,3,0:T(8,128)(2,1)} %fusion.23, bf16[9,64,64]{2,1,0:T(8,128)(2,1)S(1)} %copy-done), kind=kOutput, calls=%fused_computation.2 | convolution fusion | flops 1246003200 | bytes 23868928 | tf_op jit(solution)/shard_map/poc,bpoij->bcij/dot_general | solution.py:67
  166.5 10.8 %copy.667 = f32[130,130,64]{0,2,1:T(8,128)} copy(f32[130,130,64]{1,2,0:T(8,128)} %bitcast.344) | data formatting | bytes 8652800 | tf_op jit(solution)/shard_map/poc,bpoij->bcij/dot_general | solution.py:67
  177.3 4.1 bitcast_convert_fusion.1
  184.3 3.7 copy.668
  189.0 14.4 %all_gather.11 = bf16[16,1,64,128]{3,2,1,0:T(8,128)(2,1)S(1)} all-gather(bf16[4,1,64,128]{3,2,1,0:T(8,128)(2,1)S(1)} %pad_maximum_fusion.1), channel_id=1, replica_groups=mesh['groups'=2,'tile'=4,'chan'=2,'sub'=2] {'tile'}, dimensions={0}, use_global_device_ids=true | all-gather | bytes 327680 | tf_op jit(solution)/shard_map/all_gather | solution.py:129
  204.1 6.5 %slice.631 = f32[1,64,128,128]{2,1,3,0:T(8,128)} slice(f32[1,64,130,130]{2,1,3,0:T(8,128)} %bitcast.342), slice={[0:1], [0:64], [1:129], [1:129]} | slice | bytes 8388608 | tf_op jit(solution)/shard_map/slice | solution.py:130
  210.8 4.8 copy.672
  215.7 6.7 %slice_add_fusion.1 = f32[1,64,1,128]{2,1,3,0:T(8,128)} fusion(f32[1,64,1,128]{2,1,3,0:T(8,128)} %copy.672, f32[1,64,130,130]{2,1,3,0:T(8,128)} %bitcast.343), kind=kLoop, calls=%fused_computation.37 | loop fusion | flops 8192 | bytes 98304 | tf_op jit(solution)/shard_map/add | solution.py:40
  222.4 11.3 %scatter-add.14 = f32[1,64,128,128]{2,1,3,0:T(8,128)} dynamic-update-slice(f32[1,64,128,128]{2,1,3,0:T(8,128)} %slice.631, f32[1,64,1,128]{2,1,3,0:T(8,128)} %slice_add_fusion.1, s32[]{:T(128)} %constant.343.clone.1, s32[]{:T(128)} %constant.343.clone.1, s32[]{:T(128)} %constant.343.clone.1, s32[]{:T(128)} %constant.343.clone.1) | dynamic-update-slice | bytes 65540 | tf_op jit(solution)/shard_map/scatter-add | solution.py:40
  235.0 5.3 slice.643
  240.3 5.5 copy.674
  245.8 3.7 copy.673
  249.5 4.4 copy.675
  254.6 6.8 %slice_add_fusion = f32[1,64,128,1]{3,1,2,0:T(8,128)} fusion(f32[1,64,128,1]{3,1,2,0:T(8,128)} %copy.675, f32[1,64,128,128]{3,1,2,0:T(8,128)} %fusion.94), kind=kLoop, calls=%fused_computation.36 | loop fusion | flops 8192 | bytes 98304 | tf_op jit(solution)/shard_map/add | solution.py:43
  261.3 11.3 %scatter-add.19 = f32[1,64,128,128]{3,1,2,0:T(8,128)} dynamic-update-slice(f32[1,64,128,128]{3,1,2,0:T(8,128)} %fusion.94, f32[1,64,128,1]{3,1,2,0:T(8,128)} %slice_add_fusion, s32[]{:T(128)} %constant.343.clone.1, s32[]{:T(128)} %constant.343.clone.1, s32[]{:T(128)} %constant.343.clone.1, s32[]{:T(128)} %constant.343.clone.1) | dynamic-update-slice | bytes 65540 | tf_op jit(solution)/shard_map/scatter-add | solution.py:43
  273.2 3.7 copy_bitcast_fusion
  278.9 4.8 copy.633
  283.7 58.5 %gather_fusion.1 = bf16[16384,3]{1,0:T(8,128)(2,1)} fusion(bf16[3,24576]{0,1:T(8,128)(2,1)} %bitcast.346, s32[16384]{0:T(1024)S(1)} %fusion.92), kind=kCustom, calls=%fused_computation.1 | custom fusion | bytes 262144 | tf_op jit(solution)/shard_map/jit(_take)/gather | solution.py:102
  342.2 3.7 copy.686
  346.4 13.1 %all_gather.9 = bf16[16,1,3,128]{3,2,1,0:T(4,128)(2,1)S(1)} all-gather(bf16[4,1,3,128]{3,2,1,0:T(4,128)(2,1)S(1)} %pad_maximum_fusion.2), channel_id=1, replica_groups=mesh['groups'=2,'tile'=4,'chan'=2,'sub'=2] {'tile'}, dimensions={0}, use_global_device_ids=true | all-gather | bytes 15360 | tf_op jit(solution)/shard_map/all_gather | solution.py:107
  366.3 4.1 stack.145
  370.4 3.4 fusion.27
  376.0 3.6 pad.54
  379.6 3.7 copy.651
  385.7 13.9 %all_gather.10 = bf16[16,1,64,128]{3,2,1,0:T(8,128)(2,1)S(1)} all-gather(bf16[4,1,64,128]{3,2,1,0:T(8,128)(2,1)S(1)} %pad_maximum_fusion), channel_id=1, replica_groups=mesh['groups'=2,'tile'=4,'chan'=2,'sub'=2] {'tile'}, dimensions={0}, use_global_device_ids=true | all-gather | bytes 327680 | tf_op jit(solution)/shard_map/all_gather | solution.py:116
  400.0 4.1 copy.654
  404.1 3.2 copy.655
  407.3 2.8 scatter.34
  410.2 16.5 %scatter.35 = bf16[1,64,130,130]{3,1,2,0:T(8,128)(2,1)} dynamic-update-slice(bf16[1,64,130,130]{3,1,2,0:T(8,128)(2,1)} %scatter.34, bf16[1,64,128,1]{3,1,2,0:T(8,128)(2,1)} %copy.654, s32[]{:T(128)} %constant.343.clone.1, s32[]{:T(128)} %constant.343.clone.1, s32[]{:T(128)} %constant.352.clone.1, s32[]{:T(128)} %constant.353.clone.1) | dynamic-update-slice | bytes 32772 | tf_op jit(solution)/shard_map/scatter | solution.py:33
  428.2 10.6 %scatter.39 = bf16[1,64,130,130]{3,1,2,0:T(8,128)(2,1)} dynamic-update-slice(bf16[1,64,130,130]{3,1,2,0:T(8,128)(2,1)} %scatter.36, bf16[1,64,128,1]{3,1,2,0:T(8,128)(2,1)S(1)} %copy.655, s32[]{:T(128)} %constant.343.clone.1, s32[]{:T(128)} %constant.343.clone.1, s32[]{:T(128)} %constant.352.clone.1, s32[]{:T(128)} %constant.343.clone.1) | dynamic-update-slice | bytes 32772 | tf_op jit(solution)/shard_map/scatter | solution.py:35
  440.7 3.6 fusion.40
  452.6 4.1 fusion.47
  456.7 5.8 %fusion.63 = f32[9,64,64]{1,2,0:T(8,128)} fusion(bf16[64,128,128]{2,1,0:T(8,128)(2,1)S(1)} %bitcast.350, bf16[1,9,64,128,128]{4,2,3,1,0:T(8,128)(2,1)S(1)} %fusion.33), kind=kOutput, calls=%fused_computation.81 | convolution fusion | flops 1207996416 | bytes 21118976 | tf_op jit(solution)/shard_map/boij,bpcij->poc/dot_general | solution.py:62
  462.5 5.9 %fusion.78 = f32[9,64,3]{1,0,2:T(8,128)S(1)} fusion(f32[1,64,128,128]{3,1,2,0:T(8,128)} %scatter-add.19, f32[128,128,64,1]{1,2,3,0:T(8,128)} %get-tuple-element.234, bf16[1,9,3,128,128]{4,1,2,3,0:T(8,128)(2,1)} %copy-done.4), kind=kOutput, calls=%fused_computation.84 | convolution fusion | flops 66062016 | bytes 9280256 | tf_op jit(solution)/shard_map/boij,bpcij->poc/dot_general | solution.py:62
  468.5 57.9 %psum.14 = f32[9,64,3]{1,0,2:T(8,128)S(1)} all-reduce(f32[9,64,3]{1,0,2:T(8,128)S(1)} %fusion.78), channel_id=1, replica_groups=mesh['groups'=2,'tile'=4,'chan'=2,'sub'=2] {'tile','chan','sub'}, use_global_device_ids=true, to_apply=%region_2.3 | all-reduce | flops 1728 | bytes 13824 | tf_op jit(solution)/shard_map/psum | solution.py:134
  528.7 25.5 %all-reduce.6.cloned.1.call-done = f32[9,64,64]{1,2,0:T(8,128)} async-done(((f32[9,64,64]{1,2,0:T(8,128)}), f32[9,64,64]{1,2,0:T(8,128)}) %all-reduce.6.cloned.1.call-update) | async-done | bytes 147472 | tf_op jit(solution)/shard_map/psum | solution.py:134
  (108 shorter events, 46.1 us)
Async XLA Ops:
  7.2 139.9 %copy-start = (bf16[9,64,64]{2,1,0:T(8,128)(2,1)S(1)}, bf16[9,64,64]{2,1,0:T(8,128)(2,1)}, u32[]{:S(2)}) copy-start(bf16[9,64,64]{2,1,0:T(8,128)(2,1)} %param.38) | copy-start | bytes 221188
  18.5 98.0 %copy-start.2 = (bf16[1,64,16384]{2,1,0:T(8,128)(2,1)S(1)}, bf16[1,64,16384]{2,1,0:T(8,128)(2,1)}, u32[]{:S(2)}) copy-start(bf16[1,64,16384]{2,1,0:T(8,128)(2,1)} %param.39) | copy-start | bytes 6291460
  110.0 169.0 %all-to-all-start = ((bf16[1,3,4,6144]{3,1,0,2:T(4,128)(2,1)}), bf16[1,3,4,6144]{3,1,0,2:T(4,128)(2,1)S(1)}, u32[]{:S(2)}, u32[]{:S(2)}) async-start(bf16[1,3,4,6144]{3,1,0,2:T(4,128)(2,1)} %broadcast_select_fusion), calls=%async_computation | async-start | bytes 393216 | tf_op jit(solution)/shard_map/all_to_all | solution.py:101
  116.3 437.8 %all-reduce.6.cloned.1.call-start = ((), (), s32[]{:S(2)}) async-start(), calls=%async_computation.1 | async-start | bytes 589824 | tf_op jit(solution)/shard_map/psum | solution.py:134
  181.4 22.0 %copy-start.6 = (s32[4,4]{1,0:T(4,128)S(1)}, s32[4,4]{1,0:T(4,128)}, u32[]{:S(2)}) copy-start(s32[4,4]{1,0:T(4,128)} %param.35) | copy-start | bytes 196
  181.4 22.0 %copy-start.7 = (s32[4,4]{1,0:T(4,128)S(1)}, s32[4,4]{1,0:T(4,128)}, u32[]{:S(2)}) copy-start(s32[4,4]{1,0:T(4,128)} %param.36) | copy-start | bytes 196
  261.3 11.3 %copy-start.5 = (s32[16384]{0:T(1024)S(1)}, s32[16384]{0:T(1024)}, u32[]{:S(2)}) copy-start(s32[16384]{0:T(1024)} %param.34) | copy-start | bytes 196612
  360.1 10.3 %copy-start.8 = (bf16[9,64,3]{1,2,0:T(4,128)(2,1)S(1)}, bf16[9,64,3]{1,2,0:T(4,128)(2,1)}, u32[]{:S(2)}) copy-start(bf16[9,64,3]{1,2,0:T(4,128)(2,1)} %param.37) | copy-start | bytes 10372
  370.4 3.4 copy-start.4
  438.8 5.5 copy-start.1
  452.5 4.2 copy-start.3
Sparse Core Ops, SparseCore 0:
  462.7 91.4 all-reduce.5
where the time goes:
time: 568 us; the launch traced here: 563 us
  local copies, waits for them, and re-layouts  351 us (62%)
  blocking collectives  99.3 us (17%)
  matrix products  39.4 us (7%)
  other arithmetic  26.4 us (5%)
  waiting for transfers between devices  25.5 us (4%)
  between operations  14.8 us (3%)
  starting transfers between devices  6.51 us (1%)
    gather x2, local copies, waits for them, and re-layouts, body(): jnp.take(extended, send_pick, axis=2)  90.6 us
    gather x2, local copies, waits for them, and re-layouts, body(): jnp.take(arrived.reshape(map_count, input_count, tile_count * block_slots...  62.2 us
    psum x1, blocking collectives, body(): lax.psum((first_term, second_term), ('tile', 'chan', 'sub'))  57.9 us
    unnamed x41, local copies, waits for them, and re-layouts  49.3 us
    another operation x18, local copies, waits for them, and re-layouts  26.9 us
    psum x1, waiting for transfers between devices, body(): lax.psum((first_term, second_term), ('tile', 'chan', 'sub'))  25.5 us
    dot_general x1, matrix products, spread(): jnp.einsum('poc,bpoij->bcij', weights, windows(wide, SIDE + 2, 2), prefer...  19.4 us
    scatter x2, local copies, waits for them, and re-layouts, with_rims(): padded = padded.at[:, :, 1:-1, -1].set(incoming[1])  17.6 us
  transfers between devices with their start and end apart: 2, of which 1 were waited for; matrix products, arithmetic and copies ran while one was open for 28% of the time, Pallas kernels for 0%

commit v1 on v0

v1 whole, which is shorter than its diff:
```python
import functools
import math

import jax
import jax.numpy as jnp
from jax import lax
from jax.experimental import pallas as pl
from jax.experimental.pallas import tpu as pltpu
from jax.sharding import PartitionSpec as P

SIDE = 128
CH = 64
CIN = 3
PIX = SIDE * SIDE
ROWS = 16
STEP = ROWS * SIDE
STEPS = SIDE // ROWS
SEND_DEPTH = 256
SLOT_DEPTH = 384
MESH = pl.DeviceIdType.MESH
F32 = jnp.float32
BF16 = jnp.bfloat16
NT = (((1,), (1,)), ((), ()))


def dot(a, b):
    return jnp.dot(a, b, preferred_element_type=F32)


def dot_nt(a, b):
    return lax.dot_general(a, b, NT, preferred_element_type=F32)


def lanes(shape):
    return lax.broadcasted_iota(jnp.int32, shape, 1) % SIDE


def from_left(x):
    rows = x.shape[1] // SIDE
    out = jnp.concatenate(
        [pltpu.roll(x[:, r * SIDE : (r + 1) * SIDE], 1, 1) for r in range(rows)], axis=1
    )
    return jnp.where(lanes(x.shape) == 0, 0.0, out)


def from_right(x):
    rows = x.shape[1] // SIDE
    out = jnp.concatenate(
        [pltpu.roll(x[:, r * SIDE : (r + 1) * SIDE], SIDE - 1, 1) for r in range(rows)], axis=1
    )
    return jnp.where(lanes(x.shape) == SIDE - 1, 0.0, out)


def one_hot(depth, index):
    shape = (depth, index.shape[1])
    position = lax.broadcasted_iota(jnp.int32, shape, 0)
    return jnp.where(position == index, 1.0, 0.0).astype(BF16)


def kernel(
    tile_count,
    chan_count,
    sub_count,
    cap,
    scale,
    table_ref,
    send_ref,
    recv_ref,
    nbr_ref,
    face_ref,
    w_first_ref,
    w_fwd_ref,
    w_bwd_ref,
    w_west_ref,
    w_east_ref,
    cot_ref,
    out_ref,
    ghid_ref,
    gfirst_ref,
    gsecond_ref,
    edge,
    cc,
    hh,
    xx,
    tiles,
    slope,
    hgrad,
    grads,
    slots,
    block_out,
    block_in,
    strip_in,
    strip_hid,
    strip_rim,
    red_src,
    red_in,
    red_out,
    px_send,
    px_recv,
    in_send,
    in_recv,
    hid_send,
    hid_recv,
    rim_send,
    rim_recv,
    part_send,
    part_recv,
    sum_send,
    sum_recv,
):
    me = lax.axis_index("tile")
    group = tile_count * chan_count * sub_count
    flat = (me * chan_count + lax.axis_index("chan")) * sub_count + lax.axis_index("sub")
    groups_per_block = cap // SLOT_DEPTH
    block_rows = block_out.shape[1]

    def member(index):
        return {
            "tile": index // (chan_count * sub_count),
            "chan": (index // sub_count) % chan_count,
            "sub": index % sub_count,
        }

    barrier = pltpu.get_barrier_semaphore()

    def greet(k, carry):
        pl.semaphore_signal(
            barrier, inc=1, device_id=member((flat + k) % group), device_id_type=MESH
        )
        return carry

    lax.fori_loop(1, group, greet, 0)

    def tile_copy(src, dst, send_sem, recv_sem, peer, place):
        return pltpu.make_async_remote_copy(
            src_ref=src,
            dst_ref=dst.at[place],
            send_sem=send_sem.at[peer],
            recv_sem=recv_sem.at[place],
            device_id={"tile": peer},
            device_id_type=MESH,
        )

    def post(source, dst, send_sem, recv_sem):
        def go(k, carry):
            peer = (me + k) % tile_count
            tile_copy(source(peer), dst, send_sem, recv_sem, peer, me).start()
            return carry

        lax.fori_loop(1, tile_count, go, 0)

    def collect(source, dst, send_sem, recv_sem):
        def go(k, carry):
            peer = (me + k) % tile_count
            tile_copy(source(peer), dst, send_sem, recv_sem, peer, peer).wait_recv()
            return carry

        lax.fori_loop(1, tile_count, go, 0)

    def finish(source, dst, send_sem, recv_sem):
        def go(k, carry):
            peer = (me + k) % tile_count
            tile_copy(source(peer), dst, send_sem, recv_sem, peer, me).wait_send()
            return carry

        lax.fori_loop(1, tile_count, go, 0)

    px = (lambda peer: block_out.at[peer], block_in, px_send, px_recv)
    inp = (lambda peer: strip_in.at[me], strip_in, in_send, in_recv)
    hid = (lambda peer: strip_hid.at[me], strip_hid, hid_send, hid_recv)
    rim = (lambda peer: strip_rim.at[me], strip_rim, rim_send, rim_recv)

    flip = jnp.where(
        lax.broadcasted_iota(jnp.int32, (SIDE, SIDE), 0)
        + lax.broadcasted_iota(jnp.int32, (SIDE, SIDE), 1)
        == SIDE - 1,
        1.0,
        0.0,
    ).astype(BF16)

    def reverse(strip):
        return dot(strip.astype(BF16), flip)

    edge[...] = jnp.zeros_like(edge)
    row_of = lax.broadcasted_iota(jnp.int32, (ROWS, STEP), 0)
    cell_of = lax.broadcasted_iota(jnp.int32, (ROWS, STEP), 1)
    edge[SIDE : SIDE + ROWS, :] = jnp.where(cell_of == row_of * SIDE, 1.0, 0.0).astype(BF16)
    edge[3 * SIDE : 3 * SIDE + ROWS, :] = jnp.where(
        cell_of == row_of * SIDE + SIDE - 1, 1.0, 0.0
    ).astype(BF16)

    def west(step):
        return edge[pl.ds(pl.multiple_of(SIDE - ROWS * step, ROWS), SIDE), :]

    def east(step):
        return edge[pl.ds(pl.multiple_of(3 * SIDE - ROWS * step, ROWS), SIDE), :]

    def both(step):
        return jnp.concatenate([west(step), east(step)], axis=0)

    def cells(step, extra=0, rows=ROWS):
        return pl.ds(pl.multiple_of(step * STEP + extra * SIDE, SIDE), rows * SIDE)

    if block_rows != CIN * groups_per_block:
        slots[...] = jnp.zeros_like(slots)
    quads = groups_per_block // 4
    width = 4 * SLOT_DEPTH
    table_groups = PIX // SEND_DEPTH

    def fill(it, carry):
        pick = send_ref[0:1, pl.ds(pl.multiple_of(it * width, SIDE), width)]
        hot = one_hot(SEND_DEPTH, pick & (SEND_DEPTH - 1))
        found = dot(table_ref[...], hot)
        mask = lax.broadcasted_iota(jnp.int32, (table_groups, width), 0) == pick // SEND_DEPTH
        dest = it // quads
        first = (it % quads) * 4
        for c in range(CIN):
            part = found[c * table_groups : (c + 1) * table_groups]
            value = jnp.sum(jnp.where(mask, part, 0.0), axis=0, keepdims=True)
            for q in range(4):
                slots[dest, pl.ds(c * groups_per_block + first + q, 1), :] = value[
                    :, q * SLOT_DEPTH : (q + 1) * SLOT_DEPTH
                ]
        return carry

    lax.fori_loop(0, tile_count * quads, fill, 0)
    block_out[...] = slots[...].astype(BF16)
    block_in[me] = block_out[me]
    pl.semaphore_wait(barrier, group - 1)
    post(*px)

    cc[:, 0 : 2 * SIDE] = jnp.zeros((3 * CH, 2 * SIDE), BF16)
    cc[:, (SIDE + 2) * SIDE : (SIDE + 4) * SIDE] = jnp.zeros((3 * CH, 2 * SIDE), BF16)

    def shift_cotangent(step, columns):
        narrow = cot_ref[0, :, cells(step)]
        wide = narrow.astype(F32)
        at = cells(step, 2)
        cc[0:CH, at] = from_right(wide).astype(BF16)
        cc[CH : 2 * CH, at] = narrow
        cc[2 * CH : 3 * CH, at] = from_left(wide).astype(BF16)
        return columns + dot_nt(narrow, both(step))

    columns = lax.fori_loop(0, STEPS, shift_cotangent, jnp.zeros((CH, 2 * SIDE), F32))

    def along(column):
        return jnp.concatenate([from_right(column), column, from_left(column)], axis=0).astype(
            BF16
        )

    strip_rim[me, 0] = dot(w_bwd_ref[0:CH, :], cc[:, 2 * SIDE : 3 * SIDE]).astype(BF16)
    strip_rim[me, 1] = dot(w_east_ref[...], along(columns[:, SIDE:])).astype(BF16)
    south = dot(w_bwd_ref[2 * CH :, :], cc[:, (SIDE + 1) * SIDE : (SIDE + 2) * SIDE])
    strip_rim[me, 2] = reverse(south).astype(BF16)
    strip_rim[me, 3] = reverse(dot(w_west_ref[...], along(columns[:, :SIDE]))).astype(BF16)
    post(*rim)

    collect(*px)
    chunk = 1024

    def place(it, carry):
        at = pl.ds(pl.multiple_of(it * chunk, chunk), chunk)
        pick = recv_ref[0:1, at]
        key = ((pick // SIDE) * 171) // 512
        hot = one_hot(SLOT_DEPTH, pick - key * SLOT_DEPTH)
        table = block_in[...].reshape(tile_count * block_rows, SLOT_DEPTH)
        found = dot(table, hot)
        total = [jnp.zeros((groups_per_block, chunk), F32)] * CIN
        local = lax.broadcasted_iota(jnp.int32, (groups_per_block, chunk), 0)
        for owner in range(tile_count):
            mask = local + owner * groups_per_block == key
            for c in range(CIN):
                start = owner * block_rows + c * groups_per_block
                part = found[start : start + groups_per_block]
                total[c] = total[c] + jnp.where(mask, part, 0.0)
        row = lax.broadcasted_iota(jnp.int32, (8, chunk), 0)
        value = jnp.zeros((8, chunk), F32)
        for c in range(CIN):
            value = jnp.where(row == c, jnp.sum(total[c], axis=0, keepdims=True), value)
        tiles[:, at] = value
        return carry

    lax.fori_loop(0, PIX // chunk, place, 0)

    def tall(x):
        return jnp.concatenate([x, jnp.zeros_like(x)], axis=0)

    def tile_columns(step, total):
        return total + dot_nt(tall(tiles[:, cells(step)]).astype(BF16), both(step))

    columns = lax.fori_loop(0, STEPS, tile_columns, jnp.zeros((16, 2 * SIDE), F32))
    strip_in[me, 0] = tall(tiles[:, 0:SIDE]).astype(BF16)
    strip_in[me, 1] = columns[:, SIDE:].astype(BF16)
    strip_in[me, 2] = reverse(tall(tiles[:, PIX - SIDE : PIX])).astype(BF16)
    strip_in[me, 3] = reverse(columns[:, :SIDE]).astype(BF16)
    post(*inp)

    def interior(step, carry):
        term = dot(w_bwd_ref[...], cc[:, cells(step, 1, ROWS + 2)])
        hgrad[:, cells(step)] = (
            term[0:CH, 2 * SIDE :]
            + term[CH : 2 * CH, SIDE : SIDE + STEP]
            + term[2 * CH :, 0:STEP]
        )
        return carry

    lax.fori_loop(0, STEPS, interior, 0)

    def incoming(buffer):
        strips = []
        for k in range(4):
            near = nbr_ref[me, k]
            there = jnp.where(near >= 0, 1.0, 0.0)
            strip = buffer[jnp.maximum(near, 0), face_ref[me, k]].astype(F32) * there
            strips.append(reverse(strip) if k < 2 else strip)
        return strips

    collect(*inp)
    north, right, bottom, left = incoming(strip_in)

    def three(x, edges):
        mid = x[0:8]
        a = from_left(mid)
        b = from_right(mid)
        if edges is not None:
            a = jnp.where(lanes(a.shape) == 0, edges[0:8], a)
            b = jnp.where(lanes(b.shape) == SIDE - 1, edges[0:8], b)
        return jnp.concatenate([a + pltpu.roll(mid, 4, 0), b], axis=0).astype(BF16)

    xx[:, 0:SIDE] = three(north, None)
    xx[:, (SIDE + 1) * SIDE :] = three(bottom, None)
    sides_in = jnp.concatenate([left, right], axis=1).astype(BF16)

    def input_copies(step, carry):
        xx[:, cells(step, 1)] = three(tiles[:, cells(step)], dot(sides_in, both(step)))
        return carry

    lax.fori_loop(0, STEPS, input_copies, 0)

    def input_stack(step):
        part = xx[:, cells(step, 0, ROWS + 2)]
        return [part[:, a * SIDE : a * SIDE + STEP] for a in range(3)]

    def forward_first(step, columns):
        pre = dot(w_first_ref[...], jnp.concatenate(input_stack(step), axis=0))
        sigma = jax.nn.sigmoid(pre)
        value = pre * sigma
        slope[:, cells(step)] = sigma * (1.0 + pre * (1.0 - sigma))
        narrow = value.astype(BF16)
        at = cells(step, 1)
        hh[0:CH, at] = from_left(value).astype(BF16)
        hh[CH : 2 * CH, at] = narrow
        hh[2 * CH : 3 * CH, at] = from_right(value).astype(BF16)
        return columns + dot_nt(narrow, both(step))

    columns = lax.fori_loop(0, STEPS, forward_first, jnp.zeros((CH, 2 * SIDE), F32))
    strip_hid[me, 0] = hh[CH : 2 * CH, SIDE : 2 * SIDE]
    strip_hid[me, 1] = columns[:, SIDE:].astype(BF16)
    strip_hid[me, 2] = reverse(hh[CH : 2 * CH, PIX : PIX + SIDE]).astype(BF16)
    strip_hid[me, 3] = reverse(columns[:, :SIDE]).astype(BF16)
    post(*hid)

    collect(*rim)
    north, right, bottom, left = incoming(strip_rim)
    hgrad[:, 0:SIDE] = hgrad[:, 0:SIDE] + north
    hgrad[:, PIX - SIDE : PIX] = hgrad[:, PIX - SIDE : PIX] + bottom
    sides_rim = jnp.concatenate([left, right], axis=1).astype(BF16)
    grads[...] = jnp.zeros_like(grads)

    def backward_first(step, carry):
        total = hgrad[:, cells(step)] + dot(sides_rim, both(step))
        ghid_ref[0, :, cells(step)] = total.astype(BF16)
        pre_grad = (total * slope[:, cells(step)]).astype(BF16)
        stack = jnp.concatenate(
            [jnp.zeros((64, STEP), BF16)] + input_stack(step) + [jnp.zeros((16, STEP), BF16)],
            axis=0,
        )
        grads[0:CH, SIDE : 2 * SIDE] = grads[0:CH, SIDE : 2 * SIDE] + dot_nt(pre_grad, stack)
        return carry

    lax.fori_loop(0, STEPS, backward_first, 0)

    collect(*hid)
    north, right, bottom, left = incoming(strip_hid)

    def halo_row(strip):
        return jnp.concatenate([from_left(strip), strip, from_right(strip)], axis=0).astype(BF16)

    hh[:, 0:SIDE] = halo_row(north)
    hh[:, (SIDE + 1) * SIDE :] = halo_row(bottom)
    left = left.astype(BF16)
    right = right.astype(BF16)
    grads[0:CH, 0 : 3 * CH] = grads[0:CH, 0 : 3 * CH] + dot_nt(
        cc[CH : 2 * CH, 2 * SIDE : 3 * SIDE], hh[:, 0:SIDE]
    )
    grads[2 * CH :, 0 : 3 * CH] = grads[2 * CH :, 0 : 3 * CH] + dot_nt(
        cc[CH : 2 * CH, (SIDE + 1) * SIDE : (SIDE + 2) * SIDE], hh[:, (SIDE + 1) * SIDE :]
    )

    def backward_second(step, carry):
        at = cells(step, 1)
        hh[0:CH, at] = (hh[0:CH, at].astype(F32) + dot(left, west(step))).astype(BF16)
        hh[2 * CH :, at] = (hh[2 * CH :, at].astype(F32) + dot(right, east(step))).astype(BF16)
        part = cc[CH : 2 * CH, cells(step, 1, ROWS + 2)]
        rows = jnp.concatenate(
            [part[:, 2 * SIDE :], part[:, SIDE : SIDE + STEP], part[:, 0:STEP]], axis=0
        )
        grads[:, 0 : 3 * CH] = grads[:, 0 : 3 * CH] + dot_nt(rows, hh[:, at])
        return carry

    lax.fori_loop(0, STEPS, backward_second, 0)

    share = red_src.shape[1]
    pieces = 3 * CH // share
    for half in range(2):
        for k in range(pieces):
            red_src[half * pieces + k] = grads[
                k * share : (k + 1) * share, half * SIDE : (half + 1) * SIDE
            ]
    for k in range(2 * pieces, group):
        red_src[k] = jnp.zeros((share, SIDE), F32)

    def part_copy(peer, place):
        return pltpu.make_async_remote_copy(
            src_ref=red_src.at[peer],
            dst_ref=red_in.at[place],
            send_sem=part_send.at[peer],
            recv_sem=part_recv.at[place],
            device_id=member(peer),
            device_id_type=MESH,
        )

    def sum_copy(peer, place):
        return pltpu.make_async_remote_copy(
            src_ref=red_out.at[place],
            dst_ref=red_out.at[place],
            send_sem=sum_send.at[peer],
            recv_sem=sum_recv.at[place],
            device_id=member(peer),
            device_id_type=MESH,
        )

    def each_member(act):
        def go(k, carry):
            act((flat + k) % group)
            return carry

        lax.fori_loop(1, group, go, 0)

    red_in[flat] = red_src[flat]
    each_member(lambda peer: part_copy(peer, flat).start())

    def forward_second(step, carry):
        term = dot(w_fwd_ref[...], hh[:, cells(step, 0, ROWS + 2)])
        out_ref[0, :, cells(step)] = (
            term[0:CH, 0:STEP]
            + term[CH : 2 * CH, SIDE : SIDE + STEP]
            + term[2 * CH :, 2 * SIDE :]
        ).astype(BF16)
        return carry

    lax.fori_loop(0, STEPS // 2, forward_second, 0)
    each_member(lambda peer: part_copy(peer, peer).wait_recv())
    total = lax.fori_loop(
        0, group, lambda k, acc: acc + red_in[k], jnp.zeros((share, SIDE), F32)
    )
    red_out[flat] = total * scale
    each_member(lambda peer: sum_copy(peer, flat).start())
    lax.fori_loop(STEPS // 2, STEPS, forward_second, 0)
    each_member(lambda peer: sum_copy(peer, peer).wait_recv())

    halves = [
        jnp.concatenate([red_out[half * pieces + k] for k in range(pieces)], axis=0)
        for half in range(2)
    ]
    for a in range(3):
        rows = slice(a * CH, (a + 1) * CH)
        gsecond_ref[3 * a] = halves[0][rows, 0:CH]
        gsecond_ref[3 * a + 1] = halves[0][rows, CH : 2 * CH]
        gsecond_ref[3 * a + 2] = halves[1][rows, 0:CH]
        for b in range(3):
            lane = 64 + a * 16 + b * 4
            gfirst_ref[3 * a + b] = halves[1][0:CH, lane : lane + CIN]

    for part in (px, rim, inp, hid):
        finish(*part)
    each_member(lambda peer: part_copy(peer, flat).wait_send())
    each_member(lambda peer: sum_copy(peer, flat).wait_send())


def body(cycle_maps, send_pick, recv_pick, neighbour, facing, conv_first, conv_second, cotangent):
    tile_count = lax.axis_size("tile")
    chan_count = lax.axis_size("chan")
    sub_count = lax.axis_size("sub")
    group = tile_count * chan_count * sub_count
    cap = send_pick.shape[0] // tile_count
    scale = 1.0 / math.sqrt(group * PIX)
    table = cycle_maps.reshape(CIN * PIX // SEND_DEPTH, SEND_DEPTH)
    first = conv_first.reshape(3, 3, CH, CIN)
    first = jnp.pad(first, ((0, 0), (0, 0), (0, 0), (0, 1)))
    first = jnp.pad(first.transpose(2, 0, 1, 3).reshape(CH, 3, 12), ((0, 0), (0, 0), (0, 4)))
    first = first.reshape(CH, 48)
    second = conv_second.reshape(3, 3, CH, CH)
    w_fwd = second.transpose(0, 2, 1, 3).reshape(3 * CH, 3 * CH)
    w_bwd = second.transpose(0, 3, 1, 2).reshape(3 * CH, 3 * CH)
    w_west = second[:, 0].transpose(2, 0, 1).reshape(CH, 3 * CH)
    w_east = second[:, 2].transpose(2, 0, 1).reshape(CH, 3 * CH)
    per_block = cap // SLOT_DEPTH
    block_rows = -(-CIN * per_block // 16) * 16
    share = 8 * -(-2 * 3 * CH // (8 * group))
    vmem = pl.BlockSpec(memory_space=pltpu.VMEM)
    smem = pl.BlockSpec(memory_space=pltpu.SMEM)
    dma = pltpu.SemaphoreType.DMA
    return pl.pallas_call(
        functools.partial(kernel, tile_count, chan_count, sub_count, cap, scale),
        out_shape=(
            jax.ShapeDtypeStruct((1, CH, PIX), BF16),
            jax.ShapeDtypeStruct((1, CH, PIX), BF16),
            jax.ShapeDtypeStruct((9, CH, CIN), F32),
            jax.ShapeDtypeStruct((9, CH, CH), F32),
        ),
        in_specs=[vmem, vmem, vmem, smem, smem] + [vmem] * 6,
        out_specs=(vmem, vmem, vmem, vmem),
        scratch_shapes=[
            pltpu.VMEM((4 * SIDE, STEP), BF16),
            pltpu.VMEM((3 * CH, (SIDE + 4) * SIDE), BF16),
            pltpu.VMEM((3 * CH, (SIDE + 2) * SIDE), BF16),
            pltpu.VMEM((16, (SIDE + 2) * SIDE), BF16),
            pltpu.VMEM((8, PIX), F32),
            pltpu.VMEM((CH, PIX), F32),
            pltpu.VMEM((CH, PIX), F32),
            pltpu.VMEM((3 * CH, 2 * SIDE), F32),
            pltpu.VMEM((tile_count, block_rows, SLOT_DEPTH), F32),
            pltpu.VMEM((tile_count, block_rows, SLOT_DEPTH), BF16),
            pltpu.VMEM((tile_count, block_rows, SLOT_DEPTH), BF16),
            pltpu.VMEM((tile_count, 4, 16, SIDE), BF16),
            pltpu.VMEM((tile_count, 4, CH, SIDE), BF16),
            pltpu.VMEM((tile_count, 4, CH, SIDE), BF16),
            pltpu.VMEM((group, share, SIDE), F32),
            pltpu.VMEM((group, share, SIDE), F32),
            pltpu.VMEM((group, share, SIDE), F32),
        ]
        + [dma((tile_count,))] * 8
        + [dma((group,))] * 4,
        compiler_params=pltpu.CompilerParams(
            collective_id=0, has_side_effects=True, vmem_limit_bytes=56 * 1024 * 1024
        ),
        cost_estimate=pl.CostEstimate(
            flops=6_000_000_000, bytes_accessed=8_000_000, transcendentals=1_000_000
        ),
    )(
        table,
        send_pick.reshape(1, -1),
        recv_pick.reshape(1, -1),
        neighbour,
        facing,
        first,
        w_fwd,
        w_bwd,
        w_west,
        w_east,
        cotangent,
    )


def solution(mesh):
    in_specs = (
        P(("groups", "chan", "sub"), None, "tile"),
        P("tile"),
        P("tile"),
        P(),
        P(),
        P(),
        P(),
        P(("groups", "chan", "sub"), None, "tile"),
    )
    out_specs = (
        P(("groups", "chan", "sub"), None, "tile"),
        P(("groups", "chan", "sub"), None, "tile"),
        P("groups", None, None),
        P("groups", None, None),
    )
    return jax.shard_map(body, mesh=mesh, in_specs=in_specs, out_specs=out_specs, check_vma=False)
```

time: 568 us -> 78.4 us (0.14)
  local copies, waits for them, and re-layouts: 351 us -> 16 us
  blocking collectives: 99.3 us -> 0 us
  Pallas kernels: 0 us -> 61.3 us
  matrix products: 39.4 us -> 0 us
  other arithmetic: 26.4 us -> 0 us
  waiting for transfers between devices: 25.5 us -> 0 us
  between operations: 14.8 us -> 0.66 us
  starting transfers between devices: 6.51 us -> 0 us
    gather x4 -> x0, local copies, waits for them, and re-layouts: 153 us -> none  [the longest x2 90.6 us: body(): jnp.take(extended, send_pick, axis=2)]
    pallas_call x0 -> x1, Pallas kernels: none -> 61.3 us  [body(): pl.pallas_call(functools.partial(kernel, tile_count, chan_count, sub_coun...]
    psum x1 -> x0, blocking collectives: 57.9 us -> none  [body(): lax.psum((first_term, second_term), ('tile', 'chan', 'sub'))]
    unnamed x41 -> x7, local copies, waits for them, and re-layouts: 49.3 us -> 5.23 us
    all_gather x3 -> x0, blocking collectives: 41.5 us -> none  [the longest x1 14.4 us: body(): lax.all_gather(rim_strips, 'tile', axis=0, tiled=True)]
    another operation x36 -> x0, local copies, waits for them, and re-layouts: 39.6 us -> none
    dot_general x8 -> x0, matrix products: 39.4 us -> none  [the longest x1 19.4 us: spread(): jnp.einsum('poc,bpoij->bcij', weights, windows(wide, SIDE + 2, 2), prefer...]
    scatter x8 -> x0, local copies, waits for them, and re-layouts: 35.7 us -> none  [the longest x2 17.6 us: with_rims(): padded = padded.at[:, :, 1:-1, -1].set(incoming[1])]
  transfers between devices with their start and end apart: 2 -> 0, of which waited for: 1 -> 0; matrix products, arithmetic and copies ran while one was open for 28% -> 0% of each run, Pallas kernels for 0% -> 0%
where the time goes in v1:
time: 78.4 us; the launch traced here: 77.9 us
  Pallas kernels  61.3 us (78%)
  local copies, waits for them, and re-layouts  16 us (20%)
    pallas_call x1, Pallas kernels, body(): pl.pallas_call(functools.partial(kernel, tile_count, chan_count, sub_coun...  61.3 us
    unnamed x7, local copies, waits for them, and re-layouts  5.23 us
    reshape x2, local copies, waits for them, and re-layouts, body(): second = conv_second.reshape(3, 3, CH, CH)  2.1 us
    pallas_call x1, local copies, waits for them, and re-layouts, body(): pl.pallas_call(functools.partial(kernel, tile_count, chan_count, sub_coun...  1.71 us
    reshape x1, local copies, waits for them, and re-layouts, body(): table = cycle_maps.reshape(CIN * PIX // SEND_DEPTH, SEND_DEPTH)  1.69 us

profile of v1, /device:TPU:0, one launch (start us, length us, event | category | flops | bytes accessed | tf_op | source)
XLA Modules:
  0.0 77.9 jit_solution(10754116638699831205)
XLA Ops:
  0.6 0.7 pad_bitcast_fusion
  1.4 0.7 copy.22.w_first_ref
  2.1 1.7 %reshape.41.table_ref = bf16[192,256]{1,0:T(8,128)(2,1)} reshape(bf16[1,3,16384]{2,1,0:T(4,128)(2,1)} %param.8) | data formatting | bytes 196608 | tf_op jit(solution)/shard_map/reshape | solution.py:498
  3.8 0.8 %fusion = (bf16[3,1,64,64]{3,2,1,0:T(8,128)(2,1)S(1)}, bf16[3,1,64,64]{3,2,1,0:T(8,128)(2,1)S(1)}) fusion(bf16[3,3,64,64]{3,2,1,0:T(8,128)(2,1)} %bitcast.27), kind=kLoop, calls=%fused_computation.2 | loop fusion | bytes 98304 | tf_op jit(solution)/shard_map/slice | solution.py:507
  4.6 0.7 copy.24.w_east_ref
  5.3 0.7 copy.23.w_west_ref
  6.0 1.1 %copy.19 = bf16[3,3,64,64]{2,1,3,0:T(4,128)(2,1)S(1)} copy(bf16[3,3,64,64]{3,2,1,0:T(8,128)(2,1)} %bitcast.28) | data formatting | bytes 147456 | tf_op jit(solution)/shard_map/reshape | solution.py:503
  7.1 0.8 %reshape.49.w_bwd_ref = bf16[192,192]{1,0:T(8,128)(2,1)} reshape(bf16[3,64,3,64]{3,2,1,0:T(4,128)(2,1)S(1)} %bitcast.30) | data formatting | bytes 147456 | tf_op jit(solution)/shard_map/reshape | solution.py:505
  7.9 1.0 %copy.29 = bf16[3,3,64,64]{3,1,2,0:T(4,128)(2,1)S(1)} copy(bf16[3,3,64,64]{3,2,1,0:T(8,128)(2,1)} %bitcast.29) | data formatting | bytes 147456 | tf_op jit(solution)/shard_map/reshape | solution.py:503
  8.9 0.8 %reshape.48.w_fwd_ref = bf16[192,192]{1,0:T(8,128)(2,1)} reshape(bf16[3,64,3,64]{3,2,1,0:T(4,128)(2,1)S(1)} %bitcast.31) | data formatting | bytes 147456 | tf_op jit(solution)/shard_map/reshape | solution.py:504
  9.7 61.3 %shard_map.111 = (bf16[1,64,16384]{2,1,0:T(8,128)(2,1)}, bf16[1,64,16384]{2,1,0:T(8,128)(2,1)}, f32[9,64,3]{2,1,0:T(8,128)}, f32[9,64,64]{2,1,0:T(8,128)}) custom-call(bf16[192,256]{1,0:T(8,128)(2,1)} %reshape.41.table_ref, s32[1,24576]{1,0:T(1,128)} %bitcast.36, s32[1,16384]{1,0:T(1,128)} %bitcast.37, s32[4,4]{1,0:T(4,128)} %nbr_ref.1, s32[4,4]{1,0:T(4,128)} %face_ref.1, ...), custom_call_target="tpu_custom_call" | custom-call | flops 6000000000 | bytes 8000000 | tf_op jit(solution)/shard_map/pallas_call | solution.py:514
  71.0 1.7 %copy.25 = f32[9,64,3]{1,2,0:T(4,128)} copy(f32[9,64,3]{2,1,0:T(8,128)} %get-tuple-element.10) | data formatting | bytes 13824 | tf_op jit(solution)/shard_map/pallas_call | solution.py:514
  72.7 0.0 copy-start
  72.7 3.2 %copy.33 = bf16[1,64,16384]{2,1,0:T(8,128)(2,1)} copy(bf16[1,64,16384]{2,1,0:T(8,128)(2,1)} %get-tuple-element.18) | data formatting | bytes 4194304
  75.9 0.0 copy-done
  75.9 0.0 copy-start.1
  75.9 1.3 %copy.34 = bf16[1,64,16384]{2,1,0:T(8,128)(2,1)} copy(bf16[1,64,16384]{2,1,0:T(8,128)(2,1)S(1)} %copy-done) | data formatting | bytes 4194304
  77.2 0.0 copy-done.1
  77.2 0.7 copy.35
  (2 shorter events, 0.0 us)
Async XLA Ops:
  72.7 3.2 %copy-start = (bf16[1,64,16384]{2,1,0:T(8,128)(2,1)S(1)}, bf16[1,64,16384]{2,1,0:T(8,128)(2,1)}, u32[]{:S(2)}) copy-start(bf16[1,64,16384]{2,1,0:T(8,128)(2,1)} %get-tuple-element.19) | copy-start | bytes 6291460
  75.9 1.3 %copy-start.1 = (f32[9,64,64]{2,1,0:T(8,128)S(1)}, f32[9,64,64]{2,1,0:T(8,128)}, u32[]{:S(2)}) copy-start(f32[9,64,64]{2,1,0:T(8,128)} %get-tuple-element.21) | copy-start | bytes 442372

commit v2 on v1

--- a/solution.py
+++ b/solution.py
@@ -21,6 +21,7 @@
 F32 = jnp.float32
 BF16 = jnp.bfloat16
 NT = (((1,), (1,)), ((), ()))
+TN = (((0,), (0,)), ((), ()))
 
 
 def dot(a, b):
@@ -29,6 +30,10 @@
 
 def dot_nt(a, b):
     return lax.dot_general(a, b, NT, preferred_element_type=F32)
+
+
+def dot_tn(a, b):
+    return lax.dot_general(a, b, TN, preferred_element_type=F32)
 
 
 def lanes(shape):
@@ -53,8 +58,9 @@
 
 def one_hot(depth, index):
     shape = (depth, index.shape[1])
-    position = lax.broadcasted_iota(jnp.int32, shape, 0)
-    return jnp.where(position == index, 1.0, 0.0).astype(BF16)
+    position = lax.broadcasted_iota(jnp.int16, shape, 0)
+    hit = position == index.astype(jnp.int16)
+    return jnp.where(hit, jnp.ones(shape, BF16), jnp.zeros(shape, BF16))
 
 
 def kernel(
@@ -63,21 +69,27 @@
     sub_count,
     cap,
     scale,
-    table_ref,
+    cycle_ref,
     send_ref,
     recv_ref,
     nbr_ref,
     face_ref,
-    w_first_ref,
-    w_fwd_ref,
-    w_bwd_ref,
-    w_west_ref,
-    w_east_ref,
-    cot_ref,
+    first_ref,
+    second_ref,
+    cot_hbm,
     out_ref,
     ghid_ref,
     gfirst_ref,
     gsecond_ref,
+    w_first_ref,
+    w_fwd_ref,
+    w_bwd_ref,
+    weights,
+    table_wide,
+    table_ref,
+    cot_ref,
+    out_vmem,
+    ghid_vmem,
     edge,
     cc,
     hh,
@@ -107,6 +119,9 @@
     part_recv,
     sum_send,
     sum_recv,
+    cot_sem,
+    out_sem,
+    ghid_sem,
 ):
     me = lax.axis_index("tile")
     group = tile_count * chan_count * sub_count
@@ -130,6 +145,34 @@
         return carry
 
     lax.fori_loop(1, group, greet, 0)
+    cot_copy = pltpu.make_async_copy(cot_hbm.at[0], cot_ref, cot_sem)
+    cot_copy.start()
+
+    for a in range(3):
+        for b in range(3):
+            weights[a * CH : (a + 1) * CH, b * CH : (b + 1) * CH] = second_ref[
+                3 * a + b
+            ].astype(F32)
+    w_fwd_ref[...] = weights[0 : 3 * CH, 0 : 3 * CH].astype(BF16)
+    weights[...] = jnp.zeros_like(weights)
+    for a in range(3):
+        for b in range(3):
+            weights[b * CH : (b + 1) * CH, a * CH : (a + 1) * CH] = second_ref[
+                3 * a + b
+            ].astype(F32)
+    w_bwd_ref[...] = weights[...].T[0 : 3 * CH, 0 : 3 * CH].astype(BF16)
+    weights[0:SIDE, 0:SIDE] = jnp.zeros((SIDE, SIDE), F32)
+    for a in range(3):
+        for b in range(3):
+            at = a * 16 + b * 4
+            weights[at : at + CIN, 0:CH] = first_ref[3 * a + b].astype(F32)
+    w_first_ref[...] = weights[0:SIDE, 0:SIDE].T[0:CH, 0:48].astype(BF16)
+    for g in range(PIX // SEND_DEPTH):
+        piece = cycle_ref[0, :, g * SEND_DEPTH : (g + 1) * SEND_DEPTH].astype(F32)
+        for c in range(CIN):
+            row = c * (PIX // SEND_DEPTH) + g
+            table_wide[row : row + 1, :] = piece[c : c + 1]
+    table_ref[...] = table_wide[...].astype(BF16)
 
     def tile_copy(src, dst, send_sem, recv_sem, peer, place):
         return pltpu.make_async_remote_copy(
@@ -232,8 +275,10 @@
     cc[:, 0 : 2 * SIDE] = jnp.zeros((3 * CH, 2 * SIDE), BF16)
     cc[:, (SIDE + 2) * SIDE : (SIDE + 4) * SIDE] = jnp.zeros((3 * CH, 2 * SIDE), BF16)
 
+    cot_copy.wait()
+
     def shift_cotangent(step, columns):
-        narrow = cot_ref[0, :, cells(step)]
+        narrow = cot_ref[:, cells(step)]
         wide = narrow.astype(F32)
         at = cells(step, 2)
         cc[0:CH, at] = from_right(wide).astype(BF16)
@@ -241,19 +286,18 @@
         cc[2 * CH : 3 * CH, at] = from_left(wide).astype(BF16)
         return columns + dot_nt(narrow, both(step))
 
-    columns = lax.fori_loop(0, STEPS, shift_cotangent, jnp.zeros((CH, 2 * SIDE), F32))
-
-    def along(column):
-        return jnp.concatenate([from_right(column), column, from_left(column)], axis=0).astype(
-            BF16
-        )
-
-    strip_rim[me, 0] = dot(w_bwd_ref[0:CH, :], cc[:, 2 * SIDE : 3 * SIDE]).astype(BF16)
-    strip_rim[me, 1] = dot(w_east_ref[...], along(columns[:, SIDE:])).astype(BF16)
-    south = dot(w_bwd_ref[2 * CH :, :], cc[:, (SIDE + 1) * SIDE : (SIDE + 2) * SIDE])
-    strip_rim[me, 2] = reverse(south).astype(BF16)
-    strip_rim[me, 3] = reverse(dot(w_west_ref[...], along(columns[:, :SIDE]))).astype(BF16)
-    post(*rim)
+    cot_columns = lax.fori_loop(0, STEPS, shift_cotangent, jnp.zeros((CH, 2 * SIDE), F32))
+
+    def interior(step, carry):
+        term = dot(w_bwd_ref[...], cc[:, cells(step, 1, ROWS + 2)])
+        hgrad[:, cells(step)] = (
+            term[0:CH, 2 * SIDE :]
+            + term[CH : 2 * CH, SIDE : SIDE + STEP]
+            + term[2 * CH :, 0:STEP]
+        )
+        return carry
+
+    lax.fori_loop(0, STEPS // 2, interior, 0)
 
     collect(*px)
     chunk = 1024
@@ -295,16 +339,22 @@
     strip_in[me, 3] = reverse(columns[:, :SIDE]).astype(BF16)
     post(*inp)
 
-    def interior(step, carry):
-        term = dot(w_bwd_ref[...], cc[:, cells(step, 1, ROWS + 2)])
-        hgrad[:, cells(step)] = (
-            term[0:CH, 2 * SIDE :]
-            + term[CH : 2 * CH, SIDE : SIDE + STEP]
-            + term[2 * CH :, 0:STEP]
-        )
-        return carry
-
-    lax.fori_loop(0, STEPS, interior, 0)
+    def along(column):
+        return jnp.concatenate([from_right(column), column, from_left(column)], axis=0).astype(
+            BF16
+        )
+
+    def outer(b):
+        return jnp.concatenate([second_ref[3 * a + b] for a in range(3)], axis=0)
+
+    strip_rim[me, 0] = dot(w_bwd_ref[0:CH, :], cc[:, 2 * SIDE : 3 * SIDE]).astype(BF16)
+    strip_rim[me, 1] = dot_tn(outer(2), along(cot_columns[:, SIDE:])).astype(BF16)
+    south = dot(w_bwd_ref[2 * CH :, :], cc[:, (SIDE + 1) * SIDE : (SIDE + 2) * SIDE])
+    strip_rim[me, 2] = reverse(south).astype(BF16)
+    strip_rim[me, 3] = reverse(dot_tn(outer(0), along(cot_columns[:, :SIDE]))).astype(BF16)
+    post(*rim)
+
+    lax.fori_loop(STEPS // 2, STEPS, interior, 0)
 
     def incoming(buffer):
         strips = []
@@ -367,9 +417,18 @@
     sides_rim = jnp.concatenate([left, right], axis=1).astype(BF16)
     grads[...] = jnp.zeros_like(grads)
 
+    def ghid_copy(step):
+        at = cells(step)
+        return pltpu.make_async_copy(ghid_vmem.at[:, at], ghid_ref.at[0, :, at], ghid_sem.at[step])
+
+    def out_copy(step):
+        at = cells(step)
+        return pltpu.make_async_copy(out_vmem.at[:, at], out_ref.at[0, :, at], out_sem.at[step])
+
     def backward_first(step, carry):
         total = hgrad[:, cells(step)] + dot(sides_rim, both(step))
-        ghid_ref[0, :, cells(step)] = total.astype(BF16)
+        ghid_vmem[:, cells(step)] = total.astype(BF16)
+        ghid_copy(step).start()
         pre_grad = (total * slope[:, cells(step)]).astype(BF16)
         stack = jnp.concatenate(
             [jnp.zeros((64, STEP), BF16)] + input_stack(step) + [jnp.zeros((16, STEP), BF16)],
@@ -380,6 +439,15 @@
 
     lax.fori_loop(0, STEPS, backward_first, 0)
 
+    def backward_second(step, carry):
+        part = cc[CH : 2 * CH, cells(step, 1, ROWS + 2)]
+        rows = jnp.concatenate(
+            [part[:, 2 * SIDE :], part[:, SIDE : SIDE + STEP], part[:, 0:STEP]], axis=0
+        )
+        grads[:, 0 : 3 * CH] = grads[:, 0 : 3 * CH] + dot_nt(rows, hh[:, cells(step, 1)])
+        return carry
+
+    lax.fori_loop(0, STEPS, backward_second, 0)
     collect(*hid)
     north, right, bottom, left = incoming(strip_hid)
 
@@ -390,25 +458,16 @@
     hh[:, (SIDE + 1) * SIDE :] = halo_row(bottom)
     left = left.astype(BF16)
     right = right.astype(BF16)
+    rest = jnp.zeros((CH, SIDE), BF16)
+    grads[:, 0 : 3 * CH] = grads[:, 0 : 3 * CH] + dot_nt(
+        along(cot_columns[:, :SIDE]), jnp.concatenate([left, rest, rest], axis=0)
+    ) + dot_nt(along(cot_columns[:, SIDE:]), jnp.concatenate([rest, rest, right], axis=0))
     grads[0:CH, 0 : 3 * CH] = grads[0:CH, 0 : 3 * CH] + dot_nt(
         cc[CH : 2 * CH, 2 * SIDE : 3 * SIDE], hh[:, 0:SIDE]
     )
     grads[2 * CH :, 0 : 3 * CH] = grads[2 * CH :, 0 : 3 * CH] + dot_nt(
         cc[CH : 2 * CH, (SIDE + 1) * SIDE : (SIDE + 2) * SIDE], hh[:, (SIDE + 1) * SIDE :]
     )
-
-    def backward_second(step, carry):
-        at = cells(step, 1)
-        hh[0:CH, at] = (hh[0:CH, at].astype(F32) + dot(left, west(step))).astype(BF16)
-        hh[2 * CH :, at] = (hh[2 * CH :, at].astype(F32) + dot(right, east(step))).astype(BF16)
-        part = cc[CH : 2 * CH, cells(step, 1, ROWS + 2)]
-        rows = jnp.concatenate(
-            [part[:, 2 * SIDE :], part[:, SIDE : SIDE + STEP], part[:, 0:STEP]], axis=0
-        )
-        grads[:, 0 : 3 * CH] = grads[:, 0 : 3 * CH] + dot_nt(rows, hh[:, at])
-        return carry
-
-    lax.fori_loop(0, STEPS, backward_second, 0)
 
     share = red_src.shape[1]
     pieces = 3 * CH // share
@@ -450,13 +509,22 @@
     red_in[flat] = red_src[flat]
     each_member(lambda peer: part_copy(peer, flat).start())
 
+    def hidden_halo(step, carry):
+        at = cells(step, 1)
+        hh[0:CH, at] = (hh[0:CH, at].astype(F32) + dot(left, west(step))).astype(BF16)
+        hh[2 * CH :, at] = (hh[2 * CH :, at].astype(F32) + dot(right, east(step))).astype(BF16)
+        return carry
+
+    lax.fori_loop(0, STEPS, hidden_halo, 0)
+
     def forward_second(step, carry):
         term = dot(w_fwd_ref[...], hh[:, cells(step, 0, ROWS + 2)])
-        out_ref[0, :, cells(step)] = (
+        out_vmem[:, cells(step)] = (
             term[0:CH, 0:STEP]
             + term[CH : 2 * CH, SIDE : SIDE + STEP]
             + term[2 * CH :, 2 * SIDE :]
         ).astype(BF16)
+        out_copy(step).start()
         return carry
 
     lax.fori_loop(0, STEPS // 2, forward_second, 0)
@@ -473,6 +541,7 @@
         jnp.concatenate([red_out[half * pieces + k] for k in range(pieces)], axis=0)
         for half in range(2)
     ]
+    turned = halves[1][0:SIDE].T
     for a in range(3):
         rows = slice(a * CH, (a + 1) * CH)
         gsecond_ref[3 * a] = halves[0][rows, 0:CH]
@@ -480,12 +549,37 @@
         gsecond_ref[3 * a + 2] = halves[1][rows, 0:CH]
         for b in range(3):
             lane = 64 + a * 16 + b * 4
-            gfirst_ref[3 * a + b] = halves[1][0:CH, lane : lane + CIN]
+            gfirst_ref[3 * a + b] = turned[lane : lane + CIN, 0:CH]
 
     for part in (px, rim, inp, hid):
         finish(*part)
     each_member(lambda peer: part_copy(peer, flat).wait_send())
     each_member(lambda peer: sum_copy(peer, flat).wait_send())
+
+    def written(step, carry):
+        ghid_copy(step).wait()
+        out_copy(step).wait()
+        return carry
+
+    lax.fori_loop(0, STEPS, written, 0)
+
+
+def deliver(*refs):
+    half = (len(refs) - 1) // 2
+    sem = refs[-1]
+    copies = []
+    for src, dst in zip(refs[:half], refs[half : 2 * half]):
+        if src.shape[-1] == PIX:
+            for k in range(8):
+                at = (0, pl.ds(k // 2 * 16, 16), pl.ds(k % 2 * (PIX // 2), PIX // 2))
+                copies.append((src.at[at], dst.at[at]))
+        else:
+            copies.append((src, dst))
+    started = [pltpu.make_async_copy(a, b, sem.at[n]) for n, (a, b) in enumerate(copies)]
+    for copy in started:
+        copy.start()
+    for copy in started:
+        copy.wait()
 
 
 def body(cycle_maps, send_pick, recv_pick, neighbour, facing, conv_first, conv_second, cotangent):
@@ -495,33 +589,34 @@
     group = tile_count * chan_count * sub_count
     cap = send_pick.shape[0] // tile_count
     scale = 1.0 / math.sqrt(group * PIX)
-    table = cycle_maps.reshape(CIN * PIX // SEND_DEPTH, SEND_DEPTH)
-    first = conv_first.reshape(3, 3, CH, CIN)
-    first = jnp.pad(first, ((0, 0), (0, 0), (0, 0), (0, 1)))
-    first = jnp.pad(first.transpose(2, 0, 1, 3).reshape(CH, 3, 12), ((0, 0), (0, 0), (0, 4)))
-    first = first.reshape(CH, 48)
-    second = conv_second.reshape(3, 3, CH, CH)
-    w_fwd = second.transpose(0, 2, 1, 3).reshape(3 * CH, 3 * CH)
-    w_bwd = second.transpose(0, 3, 1, 2).reshape(3 * CH, 3 * CH)
-    w_west = second[:, 0].transpose(2, 0, 1).reshape(CH, 3 * CH)
-    w_east = second[:, 2].transpose(2, 0, 1).reshape(CH, 3 * CH)
     per_block = cap // SLOT_DEPTH
     block_rows = -(-CIN * per_block // 16) * 16
     share = 8 * -(-2 * 3 * CH // (8 * group))
     vmem = pl.BlockSpec(memory_space=pltpu.VMEM)
     smem = pl.BlockSpec(memory_space=pltpu.SMEM)
     dma = pltpu.SemaphoreType.DMA
-    return pl.pallas_call(
+    hbm = pl.BlockSpec(memory_space=pl.ANY)
+    shapes = (
+        jax.ShapeDtypeStruct((1, CH, PIX), BF16),
+        jax.ShapeDtypeStruct((1, CH, PIX), BF16),
+        jax.ShapeDtypeStruct((9, CIN, CH), F32),
+        jax.ShapeDtypeStruct((9, CH, CH), F32),
+    )
+    results = pl.pallas_call(
         functools.partial(kernel, tile_count, chan_count, sub_count, cap, scale),
-        out_shape=(
-            jax.ShapeDtypeStruct((1, CH, PIX), BF16),
-            jax.ShapeDtypeStruct((1, CH, PIX), BF16),
-            jax.ShapeDtypeStruct((9, CH, CIN), F32),
-            jax.ShapeDtypeStruct((9, CH, CH), F32),
-        ),
-        in_specs=[vmem, vmem, vmem, smem, smem] + [vmem] * 6,
-        out_specs=(vmem, vmem, vmem, vmem),
+        out_shape=shapes,
+        in_specs=[vmem, vmem, vmem, smem, smem, vmem, vmem, hbm],
+        out_specs=(hbm, hbm, vmem, vmem),
         scratch_shapes=[
+            pltpu.VMEM((CH, 48), BF16),
+            pltpu.VMEM((3 * CH, 3 * CH), BF16),
+            pltpu.VMEM((3 * CH, 3 * CH), BF16),
+            pltpu.VMEM((2 * SIDE, 2 * SIDE), F32),
+            pltpu.VMEM((CIN * PIX // SEND_DEPTH, SEND_DEPTH), F32),
+            pltpu.VMEM((CIN * PIX // SEND_DEPTH, SEND_DEPTH), BF16),
+            pltpu.VMEM((CH, PIX), BF16),
+            pltpu.VMEM((CH, PIX), BF16),
+            pltpu.VMEM((CH, PIX), BF16),
             pltpu.VMEM((4 * SIDE, STEP), BF16),
             pltpu.VMEM((3 * CH, (SIDE + 4) * SIDE), BF16),
             pltpu.VMEM((3 * CH, (SIDE + 2) * SIDE), BF16),
@@ -541,7 +636,8 @@
             pltpu.VMEM((group, share, SIDE), F32),
         ]
         + [dma((tile_count,))] * 8
-        + [dma((group,))] * 4,
+        + [dma((group,))] * 4
+        + [dma(()), dma((STEPS,)), dma((STEPS,))],
         compiler_params=pltpu.CompilerParams(
             collective_id=0, has_side_effects=True, vmem_limit_bytes=56 * 1024 * 1024
         ),
@@ -549,18 +645,24 @@
             flops=6_000_000_000, bytes_accessed=8_000_000, transcendentals=1_000_000
         ),
     )(
-        table,
+        cycle_maps,
         send_pick.reshape(1, -1),
         recv_pick.reshape(1, -1),
         neighbour,
         facing,
-        first,
-        w_fwd,
-        w_bwd,
-        w_west,
-        w_east,
+        conv_first.transpose(0, 2, 1),
+        conv_second,
         cotangent,
     )
+    out, ghid, gfirst, gsecond = pl.pallas_call(
+        deliver,
+        out_shape=shapes,
+        in_specs=[hbm] * 4,
+        out_specs=(hbm,) * 4,
+        scratch_shapes=[dma((18,))],
+        compiler_params=pltpu.CompilerParams(vmem_limit_bytes=56 * 1024 * 1024),
+    )(*results)
+    return out, ghid, gfirst.transpose(0, 2, 1), gsecond
 
 
 def solution(mesh):

time: 78.4 us -> 196 us (2.50)
  Pallas kernels: 61.3 us -> 196 us
  local copies, waits for them, and re-layouts: 16 us -> 0 us
    pallas_call x0 -> x1, Pallas kernels: none -> 138 us  [body(): pl.pallas_call(deliver, out_shape=shapes, in_specs=[hbm] * 4, out_specs=(...]
    reshape x9 -> x0, local copies, waits for them, and re-layouts: 7.52 us -> none  [the longest x2 2.1 us: body(): second = conv_second.reshape(3, 3, CH, CH)]
    unnamed x7 -> x0, local copies, waits for them, and re-layouts: 5.23 us -> none
    pallas_call x1, Pallas kernels: 61.3 us -> 57.9 us  [body(): pl.pallas_call(functools.partial(kernel, tile_count, chan_count, sub_coun...]
where the time goes in v2:
time: 196 us
  Pallas kernels  196 us (100%)
    pallas_call x1, Pallas kernels, body(): pl.pallas_call(deliver, out_shape=shapes, in_specs=[hbm] * 4, out_specs=(...  138 us
    pallas_call x1, Pallas kernels, body(): pl.pallas_call(functools.partial(kernel, tile_count, chan_count, sub_coun...  57.9 us

profile of v2, /device:TPU:0, one launch (start us, length us, event | category | flops | bytes accessed | tf_op | source)
XLA Modules:
  0.0 196.2 jit_solution(5845138542566022734)
XLA Ops:
  0.6 57.9 %shard_map.111 = (bf16[1,64,16384]{2,1,0:T(8,128)(2,1)}, bf16[1,64,16384]{2,1,0:T(8,128)(2,1)}, f32[9,3,64]{2,1,0:T(4,128)}, f32[9,64,64]{2,1,0:T(8,128)}) custom-call(bf16[1,3,16384]{2,1,0:T(4,128)(2,1)} %cycle_ref.1, s32[1,24576]{1,0:T(1,128)} %bitcast.4, s32[1,16384]{1,0:T(1,128)} %bitcast.5, s32[4,4]{1,0:T(4,128)} %nbr_ref.1, s32[4,4]{1,0:T(4,128)} %face_ref.1, ...), custom_call_target="tpu_custom_call" | custom-call | flops 6000000000 | bytes 8000000 | tf_op jit(solution)/shard_map/pallas_call | solution.py:605
  58.5 137.7 %shard_map.112 = (bf16[1,64,16384]{2,1,0:T(8,128)(2,1)}, bf16[1,64,16384]{2,1,0:T(8,128)(2,1)}, f32[9,3,64]{2,1,0:T(4,128)}, f32[9,64,64]{2,1,0:T(8,128)}) custom-call(bf16[1,64,16384]{2,1,0:T(8,128)(2,1)} %get-tuple-element.12.refs_0_, bf16[1,64,16384]{2,1,0:T(8,128)(2,1)} %get-tuple-element.13.refs_1_, f32[9,3,64]{2,1,0:T(4,128)} %get-tuple-element.14.refs_2_, ...), custom_call_target="tpu_custom_call" | custom-call | tf_op jit(solution)/shard_map/pallas_call | solution.py:657

commit v3 on v2

--- a/solution.py
+++ b/solution.py
@@ -36,24 +36,69 @@
     return lax.dot_general(a, b, TN, preferred_element_type=F32)
 
 
-def lanes(shape):
-    return lax.broadcasted_iota(jnp.int32, shape, 1) % SIDE
-
-
-def from_left(x):
-    rows = x.shape[1] // SIDE
-    out = jnp.concatenate(
-        [pltpu.roll(x[:, r * SIDE : (r + 1) * SIDE], 1, 1) for r in range(rows)], axis=1
-    )
-    return jnp.where(lanes(x.shape) == 0, 0.0, out)
-
-
-def from_right(x):
-    rows = x.shape[1] // SIDE
-    out = jnp.concatenate(
-        [pltpu.roll(x[:, r * SIDE : (r + 1) * SIDE], SIDE - 1, 1) for r in range(rows)], axis=1
-    )
-    return jnp.where(lanes(x.shape) == SIDE - 1, 0.0, out)
+def lane_is(x, lane):
+    kind = jnp.int16 if x.dtype == BF16 else jnp.int32
+    return lax.broadcasted_iota(kind, (x.shape[0], SIDE), 1) == lane
+
+
+def tile_rows(x):
+    return [x[:, r * SIDE : (r + 1) * SIDE] for r in range(x.shape[1] // SIDE)]
+
+
+def turn(x, amount):
+    return x if isinstance(amount, int) and amount % SIDE == 0 else pltpu.roll(x, amount, 1)
+
+
+def west_edge(rows, fill):
+    return [
+        jnp.where(lane_is(row, 0), jnp.zeros_like(row) if fill is None else turn(fill, (SIDE - r) % SIDE), row)
+        for r, row in enumerate(rows)
+    ]
+
+
+def east_edge(rows, fill):
+    return [
+        jnp.where(lane_is(row, SIDE - 1), jnp.zeros_like(row) if fill is None else turn(fill, SIDE - 1 - r), row)
+        for r, row in enumerate(rows)
+    ]
+
+
+def from_left(x, fill=None):
+    rows = [pltpu.roll(row, 1, 1) for row in tile_rows(x)]
+    return jnp.concatenate(west_edge(rows, fill), axis=1).astype(x.dtype)
+
+
+def from_right(x, fill=None):
+    rows = [pltpu.roll(row, SIDE - 1, 1) for row in tile_rows(x)]
+    return jnp.concatenate(east_edge(rows, fill), axis=1).astype(x.dtype)
+
+
+def unwind(strip, step):
+    return pltpu.roll(strip, (SIDE - ROWS * step) % SIDE, 1)
+
+
+def pick_edges(x, step):
+    first = jnp.zeros((x.shape[0], SIDE), x.dtype)
+    last = first
+    for r, row in enumerate(tile_rows(x)):
+        here = lane_is(row, r)
+        first = jnp.where(here, turn(row, r), first)
+        last = jnp.where(here, turn(row, r + 1), last)
+    return pltpu.roll(first, ROWS * step, 1), pltpu.roll(last, ROWS * step, 1)
+
+
+def add_edges(total, x, step):
+    first, last = pick_edges(x, step)
+    return total[0] + first, total[1] + last
+
+
+def loop(low, high, act, carry=0, unroll=2):
+    def several(k, carry):
+        for u in range(unroll):
+            carry = act(low + k * unroll + u, carry)
+        return carry
+
+    return lax.fori_loop(0, (high - low) // unroll, several, carry)
 
 
 def one_hot(depth, index):
@@ -90,7 +135,6 @@
     cot_ref,
     out_vmem,
     ghid_vmem,
-    edge,
     cc,
     hh,
     xx,
@@ -224,23 +268,6 @@
     def reverse(strip):
         return dot(strip.astype(BF16), flip)
 
-    edge[...] = jnp.zeros_like(edge)
-    row_of = lax.broadcasted_iota(jnp.int32, (ROWS, STEP), 0)
-    cell_of = lax.broadcasted_iota(jnp.int32, (ROWS, STEP), 1)
-    edge[SIDE : SIDE + ROWS, :] = jnp.where(cell_of == row_of * SIDE, 1.0, 0.0).astype(BF16)
-    edge[3 * SIDE : 3 * SIDE + ROWS, :] = jnp.where(
-        cell_of == row_of * SIDE + SIDE - 1, 1.0, 0.0
-    ).astype(BF16)
-
-    def west(step):
-        return edge[pl.ds(pl.multiple_of(SIDE - ROWS * step, ROWS), SIDE), :]
-
-    def east(step):
-        return edge[pl.ds(pl.multiple_of(3 * SIDE - ROWS * step, ROWS), SIDE), :]
-
-    def both(step):
-        return jnp.concatenate([west(step), east(step)], axis=0)
-
     def cells(step, extra=0, rows=ROWS):
         return pl.ds(pl.multiple_of(step * STEP + extra * SIDE, SIDE), rows * SIDE)
 
@@ -266,7 +293,7 @@
                 ]
         return carry
 
-    lax.fori_loop(0, tile_count * quads, fill, 0)
+    loop(0, tile_count * quads, fill)
     block_out[...] = slots[...].astype(BF16)
     block_in[me] = block_out[me]
     pl.semaphore_wait(barrier, group - 1)
@@ -279,14 +306,14 @@
 
     def shift_cotangent(step, columns):
         narrow = cot_ref[:, cells(step)]
-        wide = narrow.astype(F32)
         at = cells(step, 2)
-        cc[0:CH, at] = from_right(wide).astype(BF16)
+        cc[0:CH, at] = from_right(narrow)
         cc[CH : 2 * CH, at] = narrow
-        cc[2 * CH : 3 * CH, at] = from_left(wide).astype(BF16)
-        return columns + dot_nt(narrow, both(step))
-
-    cot_columns = lax.fori_loop(0, STEPS, shift_cotangent, jnp.zeros((CH, 2 * SIDE), F32))
+        cc[2 * CH : 3 * CH, at] = from_left(narrow)
+        return add_edges(columns, narrow, step)
+
+    none = jnp.zeros((CH, SIDE), BF16)
+    cot_columns = loop(0, STEPS, shift_cotangent, (none, none))
 
     def interior(step, carry):
         term = dot(w_bwd_ref[...], cc[:, cells(step, 1, ROWS + 2)])
@@ -297,7 +324,7 @@
         )
         return carry
 
-    lax.fori_loop(0, STEPS // 2, interior, 0)
+    loop(0, STEPS // 2, interior)
 
     collect(*px)
     chunk = 1024
@@ -324,37 +351,36 @@
         tiles[:, at] = value
         return carry
 
-    lax.fori_loop(0, PIX // chunk, place, 0)
+    loop(0, PIX // chunk, place)
 
     def tall(x):
         return jnp.concatenate([x, jnp.zeros_like(x)], axis=0)
 
     def tile_columns(step, total):
-        return total + dot_nt(tall(tiles[:, cells(step)]).astype(BF16), both(step))
-
-    columns = lax.fori_loop(0, STEPS, tile_columns, jnp.zeros((16, 2 * SIDE), F32))
+        return add_edges(total, tiles[:, cells(step)], step)
+
+    blank = jnp.zeros((8, SIDE), F32)
+    columns = loop(0, STEPS, tile_columns, (blank, blank))
     strip_in[me, 0] = tall(tiles[:, 0:SIDE]).astype(BF16)
-    strip_in[me, 1] = columns[:, SIDE:].astype(BF16)
+    strip_in[me, 1] = tall(columns[1]).astype(BF16)
     strip_in[me, 2] = reverse(tall(tiles[:, PIX - SIDE : PIX])).astype(BF16)
-    strip_in[me, 3] = reverse(columns[:, :SIDE]).astype(BF16)
+    strip_in[me, 3] = reverse(tall(columns[0])).astype(BF16)
     post(*inp)
 
     def along(column):
-        return jnp.concatenate([from_right(column), column, from_left(column)], axis=0).astype(
-            BF16
-        )
+        return jnp.concatenate([from_right(column), column, from_left(column)], axis=0)
 
     def outer(b):
         return jnp.concatenate([second_ref[3 * a + b] for a in range(3)], axis=0)
 
     strip_rim[me, 0] = dot(w_bwd_ref[0:CH, :], cc[:, 2 * SIDE : 3 * SIDE]).astype(BF16)
-    strip_rim[me, 1] = dot_tn(outer(2), along(cot_columns[:, SIDE:])).astype(BF16)
+    strip_rim[me, 1] = dot_tn(outer(2), along(cot_columns[1])).astype(BF16)
     south = dot(w_bwd_ref[2 * CH :, :], cc[:, (SIDE + 1) * SIDE : (SIDE + 2) * SIDE])
     strip_rim[me, 2] = reverse(south).astype(BF16)
-    strip_rim[me, 3] = reverse(dot_tn(outer(0), along(cot_columns[:, :SIDE]))).astype(BF16)
+    strip_rim[me, 3] = reverse(dot_tn(outer(0), along(cot_columns[0]))).astype(BF16)
     post(*rim)
 
-    lax.fori_loop(STEPS // 2, STEPS, interior, 0)
+    loop(STEPS // 2, STEPS, interior)
 
     def incoming(buffer):
         strips = []
@@ -368,24 +394,22 @@
     collect(*inp)
     north, right, bottom, left = incoming(strip_in)
 
-    def three(x, edges):
-        mid = x[0:8]
-        a = from_left(mid)
-        b = from_right(mid)
-        if edges is not None:
-            a = jnp.where(lanes(a.shape) == 0, edges[0:8], a)
-            b = jnp.where(lanes(b.shape) == SIDE - 1, edges[0:8], b)
+    def three(mid, first, last):
+        a = from_left(mid, first)
+        b = from_right(mid, last)
         return jnp.concatenate([a + pltpu.roll(mid, 4, 0), b], axis=0).astype(BF16)
 
-    xx[:, 0:SIDE] = three(north, None)
-    xx[:, (SIDE + 1) * SIDE :] = three(bottom, None)
-    sides_in = jnp.concatenate([left, right], axis=1).astype(BF16)
+    xx[:, 0:SIDE] = three(north[0:8], None, None)
+    xx[:, (SIDE + 1) * SIDE :] = three(bottom[0:8], None, None)
+    left, right = left[0:8], right[0:8]
 
     def input_copies(step, carry):
-        xx[:, cells(step, 1)] = three(tiles[:, cells(step)], dot(sides_in, both(step)))
-        return carry
-
-    lax.fori_loop(0, STEPS, input_copies, 0)
+        xx[:, cells(step, 1)] = three(
+            tiles[:, cells(step)], unwind(left, step), unwind(right, step)
+        )
+        return carry
+
+    loop(0, STEPS, input_copies)
 
     def input_stack(step):
         part = xx[:, cells(step, 0, ROWS + 2)]
@@ -398,23 +422,23 @@
         slope[:, cells(step)] = sigma * (1.0 + pre * (1.0 - sigma))
         narrow = value.astype(BF16)
         at = cells(step, 1)
-        hh[0:CH, at] = from_left(value).astype(BF16)
+        hh[0:CH, at] = from_left(narrow)
         hh[CH : 2 * CH, at] = narrow
-        hh[2 * CH : 3 * CH, at] = from_right(value).astype(BF16)
-        return columns + dot_nt(narrow, both(step))
-
-    columns = lax.fori_loop(0, STEPS, forward_first, jnp.zeros((CH, 2 * SIDE), F32))
+        hh[2 * CH : 3 * CH, at] = from_right(narrow)
+        return add_edges(columns, narrow, step)
+
+    columns = loop(0, STEPS, forward_first, (none, none))
     strip_hid[me, 0] = hh[CH : 2 * CH, SIDE : 2 * SIDE]
-    strip_hid[me, 1] = columns[:, SIDE:].astype(BF16)
+    strip_hid[me, 1] = columns[1]
     strip_hid[me, 2] = reverse(hh[CH : 2 * CH, PIX : PIX + SIDE]).astype(BF16)
-    strip_hid[me, 3] = reverse(columns[:, :SIDE]).astype(BF16)
+    strip_hid[me, 3] = reverse(columns[0]).astype(BF16)
     post(*hid)
 
     collect(*rim)
     north, right, bottom, left = incoming(strip_rim)
     hgrad[:, 0:SIDE] = hgrad[:, 0:SIDE] + north
     hgrad[:, PIX - SIDE : PIX] = hgrad[:, PIX - SIDE : PIX] + bottom
-    sides_rim = jnp.concatenate([left, right], axis=1).astype(BF16)
+    rim_west, rim_east = left, right
     grads[...] = jnp.zeros_like(grads)
 
     def ghid_copy(step):
@@ -426,7 +450,11 @@
         return pltpu.make_async_copy(out_vmem.at[:, at], out_ref.at[0, :, at], out_sem.at[step])
 
     def backward_first(step, carry):
-        total = hgrad[:, cells(step)] + dot(sides_rim, both(step))
+        rows = tile_rows(hgrad[:, cells(step)])
+        first, last = unwind(rim_west, step), unwind(rim_east, step)
+        empty = [jnp.zeros((CH, SIDE), F32)] * ROWS
+        edges = east_edge(west_edge(empty, first), last)
+        total = jnp.concatenate([row + edge for row, edge in zip(rows, edges)], axis=1)
         ghid_vmem[:, cells(step)] = total.astype(BF16)
         ghid_copy(step).start()
         pre_grad = (total * slope[:, cells(step)]).astype(BF16)
@@ -437,8 +465,6 @@
         grads[0:CH, SIDE : 2 * SIDE] = grads[0:CH, SIDE : 2 * SIDE] + dot_nt(pre_grad, stack)
         return carry
 
-    lax.fori_loop(0, STEPS, backward_first, 0)
-
     def backward_second(step, carry):
         part = cc[CH : 2 * CH, cells(step, 1, ROWS + 2)]
         rows = jnp.concatenate(
@@ -447,7 +473,7 @@
         grads[:, 0 : 3 * CH] = grads[:, 0 : 3 * CH] + dot_nt(rows, hh[:, cells(step, 1)])
         return carry
 
-    lax.fori_loop(0, STEPS, backward_second, 0)
+    loop(0, STEPS, lambda step, carry: backward_second(step, backward_first(step, carry)))
     collect(*hid)
     north, right, bottom, left = incoming(strip_hid)
 
@@ -460,8 +486,8 @@
     right = right.astype(BF16)
     rest = jnp.zeros((CH, SIDE), BF16)
     grads[:, 0 : 3 * CH] = grads[:, 0 : 3 * CH] + dot_nt(
-        along(cot_columns[:, :SIDE]), jnp.concatenate([left, rest, rest], axis=0)
-    ) + dot_nt(along(cot_columns[:, SIDE:]), jnp.concatenate([rest, rest, right], axis=0))
+        along(cot_columns[0]), jnp.concatenate([left, rest, rest], axis=0)
+    ) + dot_nt(along(cot_columns[1]), jnp.concatenate([rest, rest, right], axis=0))
     grads[0:CH, 0 : 3 * CH] = grads[0:CH, 0 : 3 * CH] + dot_nt(
         cc[CH : 2 * CH, 2 * SIDE : 3 * SIDE], hh[:, 0:SIDE]
     )
@@ -511,11 +537,13 @@
 
     def hidden_halo(step, carry):
         at = cells(step, 1)
-        hh[0:CH, at] = (hh[0:CH, at].astype(F32) + dot(left, west(step))).astype(BF16)
-        hh[2 * CH :, at] = (hh[2 * CH :, at].astype(F32) + dot(right, east(step))).astype(BF16)
-        return carry
-
-    lax.fori_loop(0, STEPS, hidden_halo, 0)
+        first = west_edge(tile_rows(hh[0:CH, at]), unwind(left, step))
+        last = east_edge(tile_rows(hh[2 * CH :, at]), unwind(right, step))
+        hh[0:CH, at] = jnp.concatenate(first, axis=1)
+        hh[2 * CH :, at] = jnp.concatenate(last, axis=1)
+        return carry
+
+    loop(0, STEPS, hidden_halo)
 
     def forward_second(step, carry):
         term = dot(w_fwd_ref[...], hh[:, cells(step, 0, ROWS + 2)])
@@ -527,14 +555,14 @@
         out_copy(step).start()
         return carry
 
-    lax.fori_loop(0, STEPS // 2, forward_second, 0)
+    loop(0, STEPS // 2, forward_second)
     each_member(lambda peer: part_copy(peer, peer).wait_recv())
     total = lax.fori_loop(
         0, group, lambda k, acc: acc + red_in[k], jnp.zeros((share, SIDE), F32)
     )
     red_out[flat] = total * scale
     each_member(lambda peer: sum_copy(peer, flat).start())
-    lax.fori_loop(STEPS // 2, STEPS, forward_second, 0)
+    loop(STEPS // 2, STEPS, forward_second)
     each_member(lambda peer: sum_copy(peer, peer).wait_recv())
 
     halves = [
@@ -565,20 +593,23 @@
 
 
 def deliver(*refs):
-    half = (len(refs) - 1) // 2
-    sem = refs[-1]
-    copies = []
-    for src, dst in zip(refs[:half], refs[half : 2 * half]):
+    count = (len(refs) - 2) // 3
+    read_sem, write_sem = refs[3 * count :]
+    reads, writes = [], []
+    for src, dst, hold in zip(refs[:count], refs[count : 2 * count], refs[2 * count : 3 * count]):
+        parts = [()]
         if src.shape[-1] == PIX:
-            for k in range(8):
-                at = (0, pl.ds(k // 2 * 16, 16), pl.ds(k % 2 * (PIX // 2), PIX // 2))
-                copies.append((src.at[at], dst.at[at]))
-        else:
-            copies.append((src, dst))
-    started = [pltpu.make_async_copy(a, b, sem.at[n]) for n, (a, b) in enumerate(copies)]
-    for copy in started:
+            parts = [(0, slice(None), pl.ds(k * STEP, STEP)) for k in range(STEPS)]
+        for at in parts:
+            a, b, c = (src.at[at], hold.at[at], dst.at[at]) if at else (src, hold, dst)
+            reads.append(pltpu.make_async_copy(a, b, read_sem.at[len(reads)]))
+            writes.append(pltpu.make_async_copy(b, c, write_sem.at[len(writes)]))
+    for copy in reads:
         copy.start()
-    for copy in started:
+    for read, write in zip(reads, writes):
+        read.wait()
+        write.start()
+    for copy in writes:
         copy.wait()
 
 
@@ -617,7 +648,6 @@
             pltpu.VMEM((CH, PIX), BF16),
             pltpu.VMEM((CH, PIX), BF16),
             pltpu.VMEM((CH, PIX), BF16),
-            pltpu.VMEM((4 * SIDE, STEP), BF16),
             pltpu.VMEM((3 * CH, (SIDE + 4) * SIDE), BF16),
             pltpu.VMEM((3 * CH, (SIDE + 2) * SIDE), BF16),
             pltpu.VMEM((16, (SIDE + 2) * SIDE), BF16),
@@ -659,7 +689,8 @@
         out_shape=shapes,
         in_specs=[hbm] * 4,
         out_specs=(hbm,) * 4,
-        scratch_shapes=[dma((18,))],
+        scratch_shapes=[pltpu.VMEM(shape.shape, shape.dtype) for shape in shapes]
+        + [dma((2 * STEPS + 2,))] * 2,
         compiler_params=pltpu.CompilerParams(vmem_limit_bytes=56 * 1024 * 1024),
     )(*results)
     return out, ghid, gfirst.transpose(0, 2, 1), gsecond

time: 196 us -> 55.1 us (0.28)
  Pallas kernels: 196 us -> 54 us
    pallas_call x1, Pallas kernels: 138 us -> 4.24 us  [body(): pl.pallas_call(deliver, out_shape=shapes, in_specs=[hbm] * 4, out_specs=(...]
    pallas_call x1, Pallas kernels: 57.9 us -> 49.8 us  [body(): pl.pallas_call(functools.partial(kernel, tile_count, chan_count, sub_coun...]
where the time goes in v3:
time: 55.1 us; the launch traced here: 54.7 us
  Pallas kernels  54 us (98%)
  between operations  0.64 us (1%)
    pallas_call x1, Pallas kernels, body(): pl.pallas_call(functools.partial(kernel, tile_count, chan_count, sub_coun...  49.8 us
    pallas_call x1, Pallas kernels, body(): pl.pallas_call(deliver, out_shape=shapes, in_specs=[hbm] * 4, out_specs=(...  4.24 us

profile of v3, /device:TPU:0, one launch (start us, length us, event | category | flops | bytes accessed | tf_op | source)
XLA Modules:
  0.0 54.7 jit_solution(598224897036450094)
XLA Ops:
  0.6 49.8 %shard_map.111 = (bf16[1,64,16384]{2,1,0:T(8,128)(2,1)}, bf16[1,64,16384]{2,1,0:T(8,128)(2,1)}, f32[9,3,64]{2,1,0:T(4,128)}, f32[9,64,64]{2,1,0:T(8,128)}) custom-call(bf16[1,3,16384]{2,1,0:T(4,128)(2,1)} %cycle_ref.1, s32[1,24576]{1,0:T(1,128)} %bitcast.4, s32[1,16384]{1,0:T(1,128)} %bitcast.5, s32[4,4]{1,0:T(4,128)} %nbr_ref.1, s32[4,4]{1,0:T(4,128)} %face_ref.1, ...), custom_call_target="tpu_custom_call" | custom-call | flops 6000000000 | bytes 8000000 | tf_op jit(solution)/shard_map/pallas_call | solution.py:636
  50.4 4.2 %shard_map.112 = (bf16[1,64,16384]{2,1,0:T(8,128)(2,1)}, bf16[1,64,16384]{2,1,0:T(8,128)(2,1)}, f32[9,3,64]{2,1,0:T(4,128)}, f32[9,64,64]{2,1,0:T(8,128)}) custom-call(bf16[1,64,16384]{2,1,0:T(8,128)(2,1)} %get-tuple-element.12.refs_0_, bf16[1,64,16384]{2,1,0:T(8,128)(2,1)} %get-tuple-element.13.refs_1_, f32[9,3,64]{2,1,0:T(4,128)} %get-tuple-element.14.refs_2_, ...), custom_call_target="tpu_custom_call" | custom-call | tf_op jit(solution)/shard_map/pallas_call | solution.py:687
